TPU v7x, 32 devices: a whole 2x2x4 slice. The times are simulated.
32 devices in a mesh: groups: 2 (over x), dev: 16 (over z, y, core).
Axes of the slice: x: 2, y: 2, z: 4, core: 2. Of those that a mesh axis runs over, the one named last changes fastest.
Arguments:
- tokens: bfloat16 [5888, 4096], P(('groups', 'dev')), parts along dimension 0, may hold values from -6 to 6
- output_cotangent: bfloat16 [5888, 1024], P(('groups', 'dev')), parts along dimension 0, may hold values from -6 to 6
- frozen_value_weight: bfloat16 [4096, 1024], replicated, may hold values from -0.09375 to 0.09375
- tenant_down_factor: bfloat16 [128, 4096, 16], P(('groups', 'dev')), parts along dimension 0, may hold values from -0.09375 to 0.09375
- tenant_up_factor: bfloat16 [128, 16, 1024], P(('groups', 'dev')), parts along dimension 0, may hold values from -1.5 to 1.5
- token_owner_device: int32 [5888, 1], P(('groups', 'dev')), parts along dimension 0, may hold values from 0 to 15; in each aligned block of 184 rows (0 to 183, 184 to 367, ...) at most 23 rows name the same one
- token_adapter_slot: int32 [5888], P(('groups', 'dev')), parts along dimension 0, may hold values from 0 to 3
Outputs:
- layer_out: bfloat16 [5888, 1024], P(('groups', 'dev')), parts along dimension 0
- grad_tokens: bfloat16 [5888, 4096], P(('groups', 'dev')), parts along dimension 0
- grad_a: bfloat16 [128, 4096, 16], P(('groups', 'dev')), parts along dimension 0
- up_factor_gradient: bfloat16 [128, 16, 1024], P(('groups', 'dev')), parts along dimension 0
There are 2 independent parts, one for each index of `groups`. A program takes and returns all parts, laid end to end along the dimension named above; an argument that names none is the same for every part. Nothing has to cross between parts.
Inputs may be any that keep to these rules, and one draw needn't show every extreme that they name: `token_owner_device`: in the tokens of one device no owner is named more than 23 times, a bound that some block reaches.
All inputs are finite; a program needn't handle non-finite values.
Results may differ from a plain program's by a relative error of at most 0.0055.
Values may be sent and summed in bfloat16 or wider, within the bound.
A program may use at most 128 MiB of HBM per device.

v0:
```python
import jax
import jax.numpy as jnp
from jax import lax
from jax.sharding import PartitionSpec as P

adapter_scale = 2.0


def frozen_products(tokens, output_cotangent, frozen_value_weight):
    frozen_output = jnp.dot(tokens, frozen_value_weight, preferred_element_type=jnp.float32)
    frozen_input_grad = lax.dot_general(
        output_cotangent,
        frozen_value_weight,
        (((1,), (1,)), ((), ())),
        preferred_element_type=jnp.float32,
    )
    return (frozen_output, frozen_input_grad)


def send_rows(send_x, send_dy, send_hot):
    return (
        lax.all_to_all(send_x, "dev", split_axis=0, concat_axis=0, tiled=True),
        lax.all_to_all(send_dy, "dev", split_axis=0, concat_axis=0, tiled=True),
        lax.all_to_all(send_hot, "dev", split_axis=0, concat_axis=0, tiled=True),
    )


def local(
    tokens,
    output_cotangent,
    frozen_value_weight,
    tenant_down_factor,
    tenant_up_factor,
    token_owner_device,
    token_adapter_slot,
):
    device_count = lax.axis_size("dev")
    row_count = tokens.shape[0]
    hidden_width = tokens.shape[1]
    output_width = output_cotangent.shape[1]
    tenant_number = tenant_down_factor.shape[0]
    adapter_rank_size = tenant_down_factor.shape[2]
    slot_capacity = 2 * row_count // device_count
    slot_total = device_count * slot_capacity
    owner_index = token_owner_device[:, 0]
    owner_hot = (owner_index[:, None] == jnp.arange(device_count, dtype=jnp.int32)[None, :]).astype(
        jnp.int32
    )
    place_index = jnp.sum((jnp.cumsum(owner_hot, axis=0) - 1) * owner_hot, axis=1)
    slot_index = owner_index * slot_capacity + place_index
    tenant_hot = (
        token_adapter_slot[:, None] == jnp.arange(tenant_number, dtype=jnp.int32)[None, :]
    ).astype(jnp.bfloat16)
    send_x = jnp.zeros((slot_total, hidden_width), jnp.bfloat16).at[slot_index].set(tokens)
    send_dy = (
        jnp.zeros((slot_total, output_width), jnp.bfloat16).at[slot_index].set(output_cotangent)
    )
    send_hot = jnp.zeros((slot_total, tenant_number), jnp.bfloat16).at[slot_index].set(tenant_hot)
    send_x = send_x.reshape(device_count, slot_capacity, hidden_width)
    send_dy = send_dy.reshape(device_count, slot_capacity, output_width)
    send_hot = send_hot.reshape(device_count, slot_capacity, tenant_number)
    frozen_output, frozen_input_grad = frozen_products(
        tokens, output_cotangent, frozen_value_weight
    )
    recv_x, recv_dy, recv_hot = send_rows(send_x, send_dy, send_hot)
    slot_input = recv_x.reshape(slot_total, hidden_width)
    slot_output_grad = recv_dy.reshape(slot_total, output_width)
    slot_hot = recv_hot.reshape(slot_total, tenant_number)
    down_factor_stack = jnp.transpose(tenant_down_factor, (1, 0, 2)).reshape(
        hidden_width, tenant_number * adapter_rank_size
    )
    up_factor_stack = tenant_up_factor.reshape(tenant_number * adapter_rank_size, output_width)
    down_parts = []
    back_parts = []
    for tenant_label in range(tenant_number):
        column_keep_mask = slot_hot[:, tenant_label : tenant_label + 1]
        down_parts.append(
            jnp.dot(
                slot_input, tenant_down_factor[tenant_label], preferred_element_type=jnp.float32
            )
            * column_keep_mask
        )
        back_part = lax.dot_general(
            slot_output_grad,
            tenant_up_factor[tenant_label],
            (((1,), (1,)), ((), ())),
            preferred_element_type=jnp.float32,
        )
        back_parts.append(back_part * column_keep_mask)
    projected_rows = jnp.concatenate(down_parts, axis=1).astype(jnp.bfloat16)
    back_rows = jnp.concatenate(back_parts, axis=1).astype(jnp.bfloat16)
    adapter_output = (
        adapter_scale * jnp.dot(projected_rows, up_factor_stack, preferred_element_type=jnp.float32)
    ).astype(jnp.bfloat16)
    adapter_input_grad = adapter_scale * lax.dot_general(
        back_rows, down_factor_stack, (((1,), (1,)), ((), ())), preferred_element_type=jnp.float32
    )
    adapter_input_grad = adapter_input_grad.astype(jnp.bfloat16)
    unclipped_down_grad = adapter_scale * lax.dot_general(
        slot_input, back_rows, (((0,), (0,)), ((), ())), preferred_element_type=jnp.float32
    )
    unclipped_up_grad = adapter_scale * lax.dot_general(
        projected_rows,
        slot_output_grad,
        (((0,), (0,)), ((), ())),
        preferred_element_type=jnp.float32,
    )
    back_y, back_dx = (
        lax.all_to_all(
            adapter_output.reshape(device_count, slot_capacity, output_width),
            "dev",
            split_axis=0,
            concat_axis=0,
            tiled=True,
        ),
        lax.all_to_all(
            adapter_input_grad.reshape(device_count, slot_capacity, hidden_width),
            "dev",
            split_axis=0,
            concat_axis=0,
            tiled=True,
        ),
    )
    row_y = back_y.reshape(slot_total, output_width)[slot_index]
    row_dx = back_dx.reshape(slot_total, hidden_width)[slot_index]
    layer_out = (frozen_output + row_y.astype(jnp.float32)).astype(jnp.bfloat16)
    grad_tokens = (frozen_input_grad + row_dx.astype(jnp.float32)).astype(jnp.bfloat16)
    local_squares = jnp.sum(unclipped_down_grad * unclipped_down_grad) + jnp.sum(
        unclipped_up_grad * unclipped_up_grad
    )
    norm_value = jnp.sqrt(lax.psum(local_squares, "dev"))
    entry_total = jnp.sqrt(
        jnp.float32(
            tenant_number * device_count * adapter_rank_size * (hidden_width + output_width)
        )
    )
    clipping_scale = jnp.minimum(jnp.float32(1.0), entry_total / (norm_value + 1e-06))
    grad_a = jnp.transpose(
        (unclipped_down_grad * clipping_scale).reshape(
            hidden_width, tenant_number, adapter_rank_size
        ),
        (1, 0, 2),
    ).astype(jnp.bfloat16)
    up_factor_gradient = (
        (unclipped_up_grad * clipping_scale)
        .reshape(tenant_number, adapter_rank_size, output_width)
        .astype(jnp.bfloat16)
    )
    return (layer_out, grad_tokens, grad_a, up_factor_gradient)


def solution(mesh):
    in_specs = (
        P(("groups", "dev"), None),
        P(("groups", "dev"), None),
        P(),
        P(("groups", "dev"), None, None),
        P(("groups", "dev"), None, None),
        P(("groups", "dev"), None),
        P(("groups", "dev")),
    )
    out_specs = (
        P(("groups", "dev"), None),
        P(("groups", "dev"), None),
        P(("groups", "dev"), None, None),
        P(("groups", "dev"), None, None),
    )
    return jax.shard_map(local, mesh=mesh, in_specs=in_specs, out_specs=out_specs, check_vma=False)
```

profile of v0, /device:TPU:0, one launch (start us, length us, event | category | flops | bytes accessed | tf_op | source)
XLA Modules:
  0.0 262.6 jit_solution(9552022251414517218)
XLA Ops:
  5.7 7.4 %all-to-all-start.1 = ((bf16[16,23,4]{1,2,0:T(4,128)(2,1)}), bf16[16,23,4]{1,2,0:T(4,128)(2,1)S(1)}, u32[]{:S(2)}, u32[]{:S(2)}) async-start(bf16[16,23,4]{1,2,0:T(4,128)(2,1)} %copy.19), calls=%async_computation.1 | async-start | bytes 32768 | tf_op jit(solution)/shard_map/all_to_all | solution.py:24
  13.1 2.1 scatter_custom_fusion.2
  16.3 3.3 %all-to-all-done.1 = bf16[16,23,4]{1,2,0:T(4,128)(2,1)S(1)} async-done(((bf16[16,23,4]{1,2,0:T(4,128)(2,1)}), bf16[16,23,4]{1,2,0:T(4,128)(2,1)S(1)}, u32[]{:S(2)}, u32[]{:S(2)}) %all-to-all-start.1) | async-done | bytes 2976 | tf_op jit(solution)/shard_map/all_to_all | solution.py:24
  19.6 4.3 %all-to-all-start.3 = ((bf16[16,23,1024]{2,1,0:T(8,128)(2,1)}), bf16[16,23,1024]{2,1,0:T(8,128)(2,1)}, u32[]{:S(2)}, u32[]{:S(2)}) async-start(bf16[16,23,1024]{2,1,0:T(8,128)(2,1)} %reshape.70), calls=%async_computation.3 | async-start | bytes 1572864 | tf_op jit(solution)/shard_map/all_to_all | solution.py:23
  23.9 4.5 %scatter_custom_fusion = bf16[368,4096]{1,0:T(8,128)(2,1)S(1)} fusion(s32[184]{0:T(256)S(1)} %bitcast.75, bf16[184,4096]{1,0:T(8,128)(2,1)} %param.7, bf16[]{:T(256)} %constant.11.clone.1), kind=kCustom, calls=%fused_computation.9 | custom fusion | bytes 3015168 | tf_op jit(solution)/shard_map/scatter | solution.py:54
  28.4 2.2 reshape.63
  30.6 12.0 %all-to-all-done.3 = bf16[16,23,1024]{2,1,0:T(8,128)(2,1)} async-done(((bf16[16,23,1024]{2,1,0:T(8,128)(2,1)}), bf16[16,23,1024]{2,1,0:T(8,128)(2,1)}, u32[]{:S(2)}, u32[]{:S(2)}) %all-to-all-start.3) | async-done | bytes 753696 | tf_op jit(solution)/shard_map/all_to_all | solution.py:23
  42.6 5.5 %all-to-all-start = ((bf16[16,23,4096]{2,1,0:T(8,128)(2,1)}), bf16[16,23,4096]{2,1,0:T(8,128)(2,1)}, u32[]{:S(2)}, u32[]{:S(2)}) async-start(bf16[16,23,4096]{2,1,0:T(8,128)(2,1)} %reshape.63), calls=%async_computation | async-start | bytes 6291456 | tf_op jit(solution)/shard_map/all_to_all | solution.py:22
  51.0 2.5 multiply_convert_fusion
  53.5 3.6 %reshape.73 = bf16[16,23,4096]{2,1,0:T(8,128)(2,1)} reshape(bf16[368,4096]{1,0:T(8,128)(2,1)} %multiply_convert_fusion) | data formatting | bytes 6029312 | tf_op jit(solution)/shard_map/reshape | solution.py:117
  57.1 50.4 %all-to-all-done = bf16[16,23,4096]{2,1,0:T(8,128)(2,1)} async-done(((bf16[16,23,4096]{2,1,0:T(8,128)(2,1)}), bf16[16,23,4096]{2,1,0:T(8,128)(2,1)}, u32[]{:S(2)}, u32[]{:S(2)}) %all-to-all-start) | async-done | bytes 3014688 | tf_op jit(solution)/shard_map/all_to_all | solution.py:22
  107.5 15.5 %all-to-all-start.4 = ((bf16[16,23,4096]{2,1,0:T(8,128)(2,1)}), bf16[16,23,4096]{2,1,0:T(8,128)(2,1)}, u32[]{:S(2)}, u32[]{:S(2)}) async-start(bf16[16,23,4096]{2,1,0:T(8,128)(2,1)} %reshape.73), calls=%async_computation.4 | async-start | bytes 6291456 | tf_op jit(solution)/shard_map/all_to_all | solution.py:116
  123.0 2.4 reshape.64
  125.4 1.6 fusion.4
  131.7 2.2 reshape.68
  133.9 3.1 %multiply_reduce_fusion = (f32[]{:T(128)}, f32[4096,64]{0,1:T(8,128)}) fusion(bf16[368,4096]{1,0:T(8,128)(2,1)S(1)} %reshape.64, bf16[368,16]{0,1:T(8,128)(2,1)} %copy-done.13, bf16[368,16]{0,1:T(8,128)(2,1)} %copy-done.12, bf16[368,16]{0,1:T(8,128)(2,1)} %copy-done.15, bf16[368,16]{0,1:T(8,128)(2,1)} %copy-done.14), kind=kOutput, calls=%fused_computation.30 | convolution fusion | flops 193912832 | bytes 4110340 | tf_op jit(solution)/shard_map/dot_general | solution.py:99
  137.0 45.4 %all-to-all-done.4 = bf16[16,23,4096]{2,1,0:T(8,128)(2,1)} async-done(((bf16[16,23,4096]{2,1,0:T(8,128)(2,1)}), bf16[16,23,4096]{2,1,0:T(8,128)(2,1)}, u32[]{:S(2)}, u32[]{:S(2)}) %all-to-all-start.4) | async-done | bytes 3014688 | tf_op jit(solution)/shard_map/all_to_all | solution.py:116
  182.4 15.5 %all-to-all-start.2 = ((bf16[16,23,1024]{2,1,0:T(8,128)(2,1)}), bf16[16,23,1024]{2,1,0:T(8,128)(2,1)}, u32[]{:S(2)}, u32[]{:S(2)}) async-start(bf16[16,23,1024]{2,1,0:T(8,128)(2,1)} %reshape.68), calls=%async_computation.2 | async-start | bytes 1572864 | tf_op jit(solution)/shard_map/all_to_all | solution.py:109
  197.9 2.0 multiply_reduce_fusion.1
  201.3 38.2 %psum.7 = f32[]{:T(128)} all-reduce(f32[]{:T(128)S(6)} %add.31), channel_id=1, replica_groups=mesh['groups'=2,'dev'=16] {'dev'}, use_global_device_ids=true, to_apply=%region_8.9 | all-reduce | flops 1 | bytes 8 | tf_op jit(solution)/shard_map/psum | solution.py:131
  241.7 2.4 reshape.74
  244.1 2.6 gather_fusion.1
  249.3 7.5 %fusion = bf16[184,4096]{1,0:T(8,128)(2,1)} fusion(bf16[184,1024]{1,0:T(8,128)(2,1)S(1)} %copy-done.24, bf16[4096,1024]{1,0:T(8,128)(2,1)} %param.9, bf16[184,4096]{1,0:T(8,128)(2,1)S(1)} %copy-done.3), kind=kOutput, calls=%fused_computation.7 | convolution fusion | flops 1545764864 | bytes 11780096 | tf_op jit(solution)/shard_map/dot_general | solution.py:11
  256.8 5.8 %fusion.3 = bf16[184,1024]{1,0:T(8,128)(2,1)} fusion(bf16[184,4096]{1,0:T(8,128)(2,1)S(1)} %copy-done.23, bf16[4096,1024]{1,0:T(8,128)(2,1)} %param.9, bf16[184,1024]{1,0:T(8,128)(2,1)S(1)} %gather_fusion), kind=kOutput, calls=%fused_computation.12 | convolution fusion | flops 1544069120 | bytes 10649600 | tf_op jit(solution)/shard_map/dot_general | solution.py:10
  (82 shorter events, 17.7 us)
Async XLA Ops:
  3.6 24.8 %copy-start.21 = (s32[184,1]{0,1:T(1,128)}, s32[184,1]{0,1:T(1,128)S(1)}, u32[]{:S(2)}) copy-start(s32[184,1]{0,1:T(1,128)S(1)} %compare_select_fusion) | copy-start | bytes 2212
  5.7 13.9 %all-to-all-start.1 = ((bf16[16,23,4]{1,2,0:T(4,128)(2,1)}), bf16[16,23,4]{1,2,0:T(4,128)(2,1)S(1)}, u32[]{:S(2)}, u32[]{:S(2)}) async-start(bf16[16,23,4]{1,2,0:T(4,128)(2,1)} %copy.19), calls=%async_computation.1 | async-start | bytes 32768 | tf_op jit(solution)/shard_map/all_to_all | solution.py:24
  19.6 23.0 %all-to-all-start.3 = ((bf16[16,23,1024]{2,1,0:T(8,128)(2,1)}), bf16[16,23,1024]{2,1,0:T(8,128)(2,1)}, u32[]{:S(2)}, u32[]{:S(2)}) async-start(bf16[16,23,1024]{2,1,0:T(8,128)(2,1)} %reshape.70), calls=%async_computation.3 | async-start | bytes 1572864 | tf_op jit(solution)/shard_map/all_to_all | solution.py:23
  30.6 19.1 %copy-start.4 = (bf16[4,16,1024]{2,1,0:T(8,128)(2,1)S(1)}, bf16[4,16,1024]{2,1,0:T(8,128)(2,1)}, u32[]{:S(2)}) copy-start(bf16[4,16,1024]{2,1,0:T(8,128)(2,1)} %param.11) | copy-start | bytes 393220
  42.6 64.9 %all-to-all-start = ((bf16[16,23,4096]{2,1,0:T(8,128)(2,1)}), bf16[16,23,4096]{2,1,0:T(8,128)(2,1)}, u32[]{:S(2)}, u32[]{:S(2)}) async-start(bf16[16,23,4096]{2,1,0:T(8,128)(2,1)} %reshape.63), calls=%async_computation | async-start | bytes 6291456 | tf_op jit(solution)/shard_map/all_to_all | solution.py:22
  48.1 2.9 %copy-start.2 = (bf16[4,4096,16]{1,2,0:T(8,128)(2,1)S(1)}, bf16[4,4096,16]{1,2,0:T(8,128)(2,1)}, u32[]{:S(2)}) copy-start(bf16[4,4096,16]{1,2,0:T(8,128)(2,1)} %param.10) | copy-start | bytes 1572868
  48.2 5.3 %copy-start.16 = (f32[368]{0:T(512)}, f32[368]{0:T(512)S(1)}, u32[]{:S(2)}) copy-start(f32[368]{0:T(512)S(1)} %get-tuple-element.6) | copy-start | bytes 4420
  48.3 5.3 %copy-start.18 = (f32[368]{0:T(512)}, f32[368]{0:T(512)S(1)}, u32[]{:S(2)}) copy-start(f32[368]{0:T(512)S(1)} %get-tuple-element.7) | copy-start | bytes 4420
  48.3 5.3 %copy-start.20 = (f32[368]{0:T(512)}, f32[368]{0:T(512)S(1)}, u32[]{:S(2)}) copy-start(f32[368]{0:T(512)S(1)} %get-tuple-element.4) | copy-start | bytes 4420
  49.7 3.9 %copy-start = (bf16[368,1024]{1,0:T(8,128)(2,1)}, bf16[368,1024]{1,0:T(8,128)(2,1)S(1)}, u32[]{:S(2)}) copy-start(bf16[368,1024]{1,0:T(8,128)(2,1)S(1)} %reshape.71) | copy-start | bytes 2260996
  50.0 7.1 %copy-start.12 = (bf16[368,16]{0,1:T(8,128)(2,1)}, bf16[368,16]{0,1:T(8,128)(2,1)S(1)}, u32[]{:S(2)}) copy-start(bf16[368,16]{0,1:T(8,128)(2,1)S(1)} %fusion.10) | copy-start | bytes 35332
  50.3 6.8 %copy-start.13 = (bf16[368,16]{0,1:T(8,128)(2,1)}, bf16[368,16]{0,1:T(8,128)(2,1)S(1)}, u32[]{:S(2)}) copy-start(bf16[368,16]{0,1:T(8,128)(2,1)S(1)} %fusion.11) | copy-start | bytes 35332
  50.6 6.5 %copy-start.14 = (bf16[368,16]{0,1:T(8,128)(2,1)}, bf16[368,16]{0,1:T(8,128)(2,1)S(1)}, u32[]{:S(2)}) copy-start(bf16[368,16]{0,1:T(8,128)(2,1)S(1)} %fusion.8) | copy-start | bytes 35332
  51.0 6.2 %copy-start.15 = (bf16[368,16]{0,1:T(8,128)(2,1)}, bf16[368,16]{0,1:T(8,128)(2,1)S(1)}, u32[]{:S(2)}) copy-start(bf16[368,16]{0,1:T(8,128)(2,1)S(1)} %fusion.9) | copy-start | bytes 35332
  107.5 74.9 %all-to-all-start.4 = ((bf16[16,23,4096]{2,1,0:T(8,128)(2,1)}), bf16[16,23,4096]{2,1,0:T(8,128)(2,1)}, u32[]{:S(2)}, u32[]{:S(2)}) async-start(bf16[16,23,4096]{2,1,0:T(8,128)(2,1)} %reshape.73), calls=%async_computation.4 | async-start | bytes 6291456 | tf_op jit(solution)/shard_map/all_to_all | solution.py:116
  133.9 64.0 %copy-start.7 = (bf16[368,16]{0,1:T(8,128)(2,1)S(1)}, bf16[368,16]{0,1:T(8,128)(2,1)}, u32[]{:S(2)}) copy-start(bf16[368,16]{0,1:T(8,128)(2,1)} %copy-done.6) | copy-start | bytes 35332
  133.9 64.0 %copy-start.9 = (bf16[368,16]{0,1:T(8,128)(2,1)S(1)}, bf16[368,16]{0,1:T(8,128)(2,1)}, u32[]{:S(2)}) copy-start(bf16[368,16]{0,1:T(8,128)(2,1)} %copy-done.8) | copy-start | bytes 35332
  133.9 64.0 %copy-start.11 = (bf16[368,16]{0,1:T(8,128)(2,1)S(1)}, bf16[368,16]{0,1:T(8,128)(2,1)}, u32[]{:S(2)}) copy-start(bf16[368,16]{0,1:T(8,128)(2,1)} %copy-done.10) | copy-start | bytes 35332
  133.9 67.4 %copy-start.22 = (s32[184,1]{0,1:T(1,128)S(1)}, s32[184,1]{0,1:T(1,128)}, u32[]{:S(2)}) copy-start(s32[184,1]{0,1:T(1,128)} %copy-done.21) | copy-start | bytes 2212
  137.0 103.8 %copy-start.1 = (f32[4096,64]{0,1:T(8,128)S(1)}, f32[4096,64]{0,1:T(8,128)}, u32[]{:S(2)}) copy-start(f32[4096,64]{0,1:T(8,128)} %get-tuple-element.9) | copy-start | bytes 3145732
  182.4 64.3 %all-to-all-start.2 = ((bf16[16,23,1024]{2,1,0:T(8,128)(2,1)}), bf16[16,23,1024]{2,1,0:T(8,128)(2,1)}, u32[]{:S(2)}, u32[]{:S(2)}) async-start(bf16[16,23,1024]{2,1,0:T(8,128)(2,1)} %reshape.68), calls=%async_computation.2 | async-start | bytes 1572864 | tf_op jit(solution)/shard_map/all_to_all | solution.py:109
  246.7 2.5 copy-start.3
  246.7 2.5 copy-start.24
  249.2 7.5 %copy-start.23 = (bf16[184,4096]{1,0:T(8,128)(2,1)S(1)}, bf16[184,4096]{1,0:T(8,128)(2,1)}, u32[]{:S(2)}) copy-start(bf16[184,4096]{1,0:T(8,128)(2,1)} %param.7) | copy-start | bytes 4521988
  (6 other events, 7.6 us)
where the time goes:
time: 264 us; the launch traced here: 263 us
  waiting for transfers between devices  111 us (42%)
  starting transfers between devices  48.1 us (18%)
  blocking collectives  38.2 us (14%)
  local copies, waits for them, and re-layouts  28.7 us (11%)
  matrix products  27.8 us (11%)
  other arithmetic  5.61 us (2%)
  between operations  3.09 us (1%)
    all_to_all x1, waiting for transfers between devices, send_rows(): lax.all_to_all(send_x, 'dev', split_axis=0, concat_axis=0, tiled=True)  50.4 us
    all_to_all x1, waiting for transfers between devices, local(): lax.all_to_all(adapter_input_grad.reshape(device_count, slot_capacity, hi...  45.4 us
    psum x1, blocking collectives, local(): norm_value = jnp.sqrt(lax.psum(local_squares, 'dev'))  38.2 us
    all_to_all x1, starting transfers between devices, local(): lax.all_to_all(adapter_input_grad.reshape(device_count, slot_capacity, hi...  15.5 us
    all_to_all x1, starting transfers between devices, local(): lax.all_to_all(adapter_output.reshape(device_count, slot_capacity, output...  15.5 us
    all_to_all x1, waiting for transfers between devices, send_rows(): lax.all_to_all(send_dy, 'dev', split_axis=0, concat_axis=0, tiled=True)  12 us
    dot_general x1, matrix products, frozen_products(): lax.dot_general(output_cotangent, frozen_value_weight, (((1,), (1,)), (()...  7.51 us
    all_to_all x1, starting transfers between devices, send_rows(): lax.all_to_all(send_hot, 'dev', split_axis=0, concat_axis=0, tiled=True)  7.39 us
  transfers between devices with their start and end apart: 5, of which 4 were waited for; matrix products, arithmetic and copies ran while one was open for 15% of the time, Pallas kernels for 0%

commit v1 on v0

v1 whole, which is shorter than its diff:
```python
import jax
import jax.numpy as jnp
from jax import lax
from jax.sharding import PartitionSpec as P

adapter_scale = 2.0
plane = 4
f32 = jnp.float32
bf16 = jnp.bfloat16


def dot_nn(a, b):
    return lax.dot_general(a, b, (((1,), (0,)), ((), ())), preferred_element_type=f32)


def dot_nt(a, b):
    return lax.dot_general(a, b, (((1,), (1,)), ((), ())), preferred_element_type=f32)


def dot_tn(a, b):
    return lax.dot_general(a, b, (((0,), (0,)), ((), ())), preferred_element_type=f32)


def local(x, dy, w, down_f, up_f, owner, slot):
    n = lax.axis_size("dev")
    me = lax.axis_index("dev")
    layers = n // plane
    tenants, hidden, rank = down_f.shape
    width = up_f.shape[2]
    cols = tenants * rank
    columns = [[z * plane + k for z in range(layers)] for k in range(plane)]
    to_core = [(i, i ^ 1) for i in range(n)]
    to_line = [(i, i ^ 2) for i in range(n)]

    def gather(v):
        return lax.all_gather(v, "dev", axis_index_groups=columns, tiled=True)

    def scatter(v):
        return lax.psum_scatter(
            v, "dev", scatter_dimension=0, axis_index_groups=columns, tiled=True
        )

    def swap_core(v):
        return lax.ppermute(v, "dev", to_core)

    def swap_line(v):
        return lax.ppermute(v, "dev", to_line)

    ids = (owner[:, 0] * tenants + slot).reshape(-1, 1)
    ids_p = swap_line(ids)
    up0 = gather(up_f.reshape(cols, width))
    dy_p = swap_line(dy)
    up1 = swap_core(up0)
    down0 = gather(jnp.transpose(down_f, (0, 2, 1)).reshape(cols, hidden))
    x_p = swap_line(x)
    down1 = swap_core(down0)

    col = jnp.arange(layers * cols, dtype=jnp.int32)[None, :]
    label0 = ((col // cols) * plane + me % plane) * tenants + (col // rank) % tenants
    label1 = label0 + jnp.where(me % 2 == 0, tenants, -tenants)
    ids_of = (ids, ids_p)
    keep = [[i == lab for lab in (label0, label1)] for i in ids_of]
    xs, dys, ups, downs = (x, x_p), (dy, dy_p), (up0, up1), (down0, down1)

    def masked(v, k):
        return jnp.where(k, v, 0.0).astype(bf16)

    back = [[masked(dot_nt(dys[r], ups[c]), keep[r][c]) for c in range(2)] for r in range(2)]
    proj = [[masked(dot_nt(xs[r], downs[c]), keep[r][c]) for c in range(2)] for r in range(2)]

    def lora(coef, factors, r):
        return (
            adapter_scale * (dot_nn(coef[r][0], factors[0]) + dot_nn(coef[r][1], factors[1]))
        ).astype(bf16)

    def partial(coef, rows, c):
        return dot_tn(coef[0][c], rows[0]) + dot_tn(coef[1][c], rows[1])

    ga = scatter(
        (partial(back, xs, 0) + swap_core(partial(back, xs, 1).astype(bf16)).astype(f32)).astype(bf16)
    )
    gb = scatter(
        (partial(proj, dys, 0) + swap_core(partial(proj, dys, 1).astype(bf16)).astype(f32)).astype(bf16)
    )
    far_dx = swap_line(lora(back, downs, 1))
    far_y = swap_line(lora(proj, ups, 1))
    near_dx = lora(back, downs, 0)
    near_y = lora(proj, ups, 0)
    layer_out = (dot_nn(x, w) + (near_y.astype(f32) + far_y.astype(f32))).astype(bf16)
    grad_tokens = (dot_nt(dy, w) + (near_dx.astype(f32) + far_dx.astype(f32))).astype(bf16)

    ga = adapter_scale * ga.astype(f32)
    gb = adapter_scale * gb.astype(f32)
    norm = jnp.sqrt(lax.psum(jnp.sum(ga * ga) + jnp.sum(gb * gb), "dev"))
    entries = jnp.sqrt(f32(tenants * n * rank * (hidden + width)))
    factor = jnp.minimum(f32(1.0), entries / (norm + 1e-06))
    grad_a = jnp.transpose((ga * factor).astype(bf16).reshape(tenants, rank, hidden), (0, 2, 1))
    grad_b = (gb * factor).astype(bf16).reshape(tenants, rank, width)
    return (layer_out, grad_tokens, grad_a, grad_b)


def solution(mesh):
    rows = P(("groups", "dev"), None)
    stack = P(("groups", "dev"), None, None)
    return jax.shard_map(
        local,
        mesh=mesh,
        in_specs=(rows, rows, P(), stack, stack, rows, P(("groups", "dev"))),
        out_specs=(rows, rows, stack, stack),
        check_vma=False,
    )
```

time: 264 us -> 212 us (0.80)
  starting transfers between devices: 48.1 us -> 6.59 us
  waiting for transfers between devices: 111 us -> 78.1 us
  local copies, waits for them, and re-layouts: 28.7 us -> 2.68 us
  matrix products: 27.8 us -> 50.9 us
  between operations: 3.09 us -> 16.2 us
  blocking collectives: 38.2 us -> 50.2 us
    all_to_all x5 -> x0, waiting for transfers between devices: 111 us -> none  [the longest x1 50.4 us: send_rows(): lax.all_to_all(send_x, 'dev', split_axis=0, concat_axis=0, tiled=True)]
    all_to_all x5 -> x0, starting transfers between devices: 48.1 us -> none  [the longest x1 15.5 us: local(): lax.all_to_all(adapter_input_grad.reshape(device_count, slot_capacity, hi...]
    ppermute x0 -> x9, waiting for transfers between devices: none -> 46.3 us  [the longest x5 46.3 us: swap_line(): return lax.ppermute(v, 'dev', to_line)]
    all_gather x0 -> x1, waiting for transfers between devices: none -> 31.1 us  [gather(): return lax.all_gather(v, 'dev', axis_index_groups=columns, tiled=True)]
    dot_general x14 -> x26, matrix products: 27.8 us -> 50.9 us  [the longest x9 19.5 us: dot_nt(): lax.dot_general(a, b, (((1,), (1,)), ((), ())), preferred_element_type=f32)]
    all_gather x0 -> x1, blocking collectives: none -> 19.2 us  [gather(): return lax.all_gather(v, 'dev', axis_index_groups=columns, tiled=True)]
    reshape x11 -> x0, local copies, waits for them, and re-layouts: 17.5 us -> none  [the longest x1 3.55 us: local(): adapter_input_grad.reshape(device_count, slot_capacity, hidden_width)]
    psum x1, blocking collectives: 38.2 us -> 31 us  [local(): norm = jnp.sqrt(lax.psum(jnp.sum(ga * ga) + jnp.sum(gb * gb), 'dev'))]
  transfers between devices with their start and end apart: 5 -> 12, of which waited for: 4 -> 3; matrix products, arithmetic and copies ran while one was open for 15% -> 24% of each run, Pallas kernels for 0% -> 0%
where the time goes in v1:
time: 212 us
  waiting for transfers between devices  78.1 us (37%)
  matrix products  50.9 us (24%)
  blocking collectives  50.2 us (24%)
  between operations  16.2 us (8%)
  other arithmetic  7.34 us (3%)
  starting transfers between devices  6.59 us (3%)
  local copies, waits for them, and re-layouts  2.68 us (1%)
    ppermute x5, waiting for transfers between devices, swap_line(): return lax.ppermute(v, 'dev', to_line)  46.3 us
    all_gather x1, waiting for transfers between devices, gather(): return lax.all_gather(v, 'dev', axis_index_groups=columns, tiled=True)  31.1 us
    psum x1, blocking collectives, local(): norm = jnp.sqrt(lax.psum(jnp.sum(ga * ga) + jnp.sum(gb * gb), 'dev'))  31 us
    dot_general x9, matrix products, dot_nt(): lax.dot_general(a, b, (((1,), (1,)), ((), ())), preferred_element_type=f32)  19.5 us
    all_gather x1, blocking collectives, gather(): return lax.all_gather(v, 'dev', axis_index_groups=columns, tiled=True)  19.2 us
    dot_general x9, matrix products, dot_nn(): lax.dot_general(a, b, (((1,), (0,)), ((), ())), preferred_element_type=f32)  18.1 us
    dot_general x8, matrix products, dot_tn(): lax.dot_general(a, b, (((0,), (0,)), ((), ())), preferred_element_type=f32)  13.2 us
    ppermute x5, starting transfers between devices, swap_line(): return lax.ppermute(v, 'dev', to_line)  5.72 us
  transfers between devices with their start and end apart: 12, of which 3 were waited for; matrix products, arithmetic and copies ran while one was open for 24% of the time, Pallas kernels for 0%

profile of v1, /device:TPU:0, one launch (start us, length us, event | category | flops | bytes accessed | tf_op | source)
XLA Modules:
  0.0 211.9 jit_solution(6592707665298893389)
XLA Ops:
  8.0 19.2 %all_gather.7 = bf16[256,1024]{1,0:T(8,128)(2,1)S(1)} all-gather(bf16[64,1024]{1,0:T(8,128)(2,1)} %bitcast.65), channel_id=1, replica_groups={{0,4,8,12},{1,5,9,13},{2,6,10,14},{3,7,11,15},{16,20,24,28},{17,21,25,2..., dimensions={0}, use_global_device_ids=true | all-gather | bytes 655360 | tf_op jit(solution)/shard_map/all_gather | solution.py:36
  27.2 1.6 collective-permute-start.3
  28.8 31.1 %all-gather.2.cloned.1.call-done = bf16[256,4096]{1,0:T(8,128)(2,1)} async-done(((bf16[64,4096]{1,0:T(8,128)(2,1)}), bf16[256,4096]{1,0:T(8,128)(2,1)}) %all-gather.2.cloned.1.call-update) | async-done | bytes 2097168 | tf_op jit(solution)/shard_map/all_gather | solution.py:36
  61.2 1.5 collective-permute-start.2
  63.3 2.0 fusion.26
  65.6 8.2 %collective-permute-done.5 = bf16[184,1024]{1,0:T(8,128)(2,1)S(1)} collective-permute-done((bf16[184,1024]{1,0:T(8,128)(2,1)}, bf16[184,1024]{1,0:T(8,128)(2,1)S(1)}, u32[]{:S(2)}, u32[]{:S(2)}) %collective-permute-start.5) | collective-permute-done | bytes 376864 | tf_op jit(solution)/shard_map/ppermute | solution.py:47
  75.4 3.7 %fusion.2 = bf16[256,4096]{1,0:T(8,128)(2,1)} fusion(f32[256,4096]{1,0:T(8,128)S(1)} %fusion.49, bf16[184,256]{1,0:T(8,128)(2,1)S(1)} %fusion.29, bf16[184,4096]{1,0:T(8,128)(2,1)} %collective-permute-done.3), kind=kOutput, calls=%fused_computation.4 | convolution fusion | flops 387973120 | bytes 7892992 | tf_op jit(solution)/shard_map/dot_general | solution.py:21
  80.0 2.5 %fusion.23 = bf16[184,256]{1,0:T(8,128)(2,1)S(1)} fusion(bf16[184,4096]{1,0:T(8,128)(2,1)S(1)} %copy-done.2, bf16[256,4096]{1,0:T(8,128)(2,1)} %collective-permute-done, s32[256]{0:T(256)S(1)} %broadcast_add_fusion, s32[184]{0:T(256)S(1)} %add.132), kind=kOutput, calls=%fused_computation.41 | convolution fusion | flops 386017280 | bytes 3700448 | tf_op jit(solution)/shard_map/dot_general | solution.py:17
  83.5 2.9 %fusion.25 = bf16[184,256]{1,0:T(8,128)(2,1)S(1)} fusion(bf16[184,4096]{1,0:T(8,128)(2,1)} %collective-permute-done.3, bf16[256,4096]{1,0:T(8,128)(2,1)} %collective-permute-done, s32[256]{0:T(256)S(1)} %broadcast_add_fusion, s32[184]{0:T(256)S(1)} %bitcast.70), kind=kOutput, calls=%fused_computation.43 | convolution fusion | flops 386017280 | bytes 3700448 | tf_op jit(solution)/shard_map/dot_general | solution.py:17
  87.7 2.2 %fusion.24 = bf16[184,256]{1,0:T(8,128)(2,1)S(1)} fusion(bf16[184,4096]{1,0:T(8,128)(2,1)} %collective-permute-done.3, bf16[256,4096]{1,0:T(8,128)(2,1)S(1)} %copy-done, s32[256]{0:T(256)S(1)} %fusion.36, s32[184]{0:T(256)S(1)} %bitcast.71), kind=kOutput, calls=%fused_computation.42 | convolution fusion | flops 386017280 | bytes 3700448 | tf_op jit(solution)/shard_map/dot_general | solution.py:17
  90.6 1.1 fusion.12
  92.0 2.2 %fusion.48 = f32[256,4096]{1,0:T(8,128)S(1)} fusion(bf16[184,256]{1,0:T(8,128)(2,1)} %fusion.26, bf16[184,4096]{1,0:T(8,128)(2,1)} %param.7), kind=kOutput, calls=%fused_computation.80 | convolution fusion | flops 385875968 | bytes 5795840 | tf_op jit(solution)/shard_map/dot_general | solution.py:21
  95.2 4.4 %fusion.1 = bf16[256,4096]{1,0:T(8,128)(2,1)} fusion(f32[256,4096]{1,0:T(8,128)S(1)} %fusion.48, bf16[184,256]{1,0:T(8,128)(2,1)S(1)} %fusion.28, bf16[184,4096]{1,0:T(8,128)(2,1)} %collective-permute-done.3, bf16[256,4096]{1,0:T(8,128)(2,1)} %collective-permute-done.7), kind=kOutput, calls=%fused_computation.3 | convolution fusion | flops 390070272 | bytes 9990144 | tf_op jit(solution)/shard_map/dot_general | solution.py:21
  99.6 8.0 %fusion.45 = f32[184,4096]{1,0:T(8,128)} fusion(bf16[184,1024]{1,0:T(8,128)(2,1)S(1)} %copy-done.5, bf16[4096,1024]{1,0:T(8,128)(2,1)} %param.9), kind=kOutput, calls=%fused_computation.77 | convolution fusion | flops 1543503872 | bytes 11780096 | tf_op jit(solution)/shard_map/dot_general | solution.py:17
  107.6 5.1 %fusion.42 = f32[184,1024]{1,0:T(8,128)S(1)} fusion(bf16[184,4096]{1,0:T(8,128)(2,1)S(1)} %copy-done.3, bf16[4096,1024]{1,0:T(8,128)(2,1)} %param.9), kind=kOutput, calls=%fused_computation.74 | convolution fusion | flops 1543503872 | bytes 10649600 | tf_op jit(solution)/shard_map/dot_general | solution.py:13
  113.7 3.4 %fusion.5 = bf16[184,4096]{1,0:T(8,128)(2,1)} fusion(f32[184,4096]{1,0:T(8,128)S(1)} %fusion.47, bf16[184,256]{1,0:T(8,128)(2,1)S(1)} %copy-done.23, bf16[256,4096]{1,0:T(8,128)(2,1)} %collective-permute-done), kind=kOutput, calls=%fused_computation.9 | convolution fusion | flops 388136960 | bytes 6713344 | tf_op jit(solution)/shard_map/dot_general | solution.py:13
  118.1 1.6 collective-permute-start.4
  120.0 2.2 %fusion.46 = f32[184,4096]{1,0:T(8,128)} fusion(bf16[184,256]{1,0:T(8,128)(2,1)S(1)} %copy-done.18, bf16[256,4096]{1,0:T(8,128)(2,1)S(1)} %copy-done), kind=kOutput, calls=%fused_computation.78 | convolution fusion | flops 385875968 | bytes 5206016 | tf_op jit(solution)/shard_map/dot_general | solution.py:13
  122.2 38.1 %collective-permute-done.4 = bf16[184,1024]{1,0:T(8,128)(2,1)S(1)} collective-permute-done((bf16[184,1024]{1,0:T(8,128)(2,1)S(1)}, bf16[184,1024]{1,0:T(8,128)(2,1)S(1)}, u32[]{:S(2)}, u32[]{:S(2)}) %collective-permute-start.4) | collective-permute-done | bytes 376864 | tf_op jit(solution)/shard_map/ppermute | solution.py:47
  161.4 1.6 fusion.34
  162.9 1.9 fusion.31
  166.2 5.0 %fusion.10 = bf16[184,4096]{1,0:T(8,128)(2,1)} fusion(f32[184,4096]{1,0:T(8,128)} %fusion.45, f32[184,4096]{1,0:T(8,128)S(1)} %copy-done.4, bf16[184,256]{1,0:T(8,128)(2,1)} %copy-done.21, bf16[256,4096]{1,0:T(8,128)(2,1)} %collective-permute-done, bf16[184,4096]{1,0:T(8,128)(2,1)} %collective-permute-done.6), kind=kOutput, calls=%fused_computation.14 | convolution fusion | flops 391905280 | bytes 11235328 | tf_op jit(solution)/shard_map/dot_general | solution.py:13
  171.2 31.0 %psum.7 = f32[]{:T(128)} all-reduce(f32[]{:T(128)S(6)} %add.155), channel_id=1, replica_groups=mesh['groups'=2,'dev'=16] {'dev'}, use_global_device_ids=true, to_apply=%region_4.5 | all-reduce | flops 1 | bytes 8 | tf_op jit(solution)/shard_map/psum | solution.py:94
  202.9 1.6 fusion.35
  (87 shorter events, 13.5 us)
Async XLA Ops:
  7.2 58.1 %copy-start.5 = (bf16[184,1024]{1,0:T(8,128)(2,1)S(1)}, bf16[184,1024]{1,0:T(8,128)(2,1)}, u32[]{:S(2)}) copy-start(bf16[184,1024]{1,0:T(8,128)(2,1)} %param.8) | copy-start | bytes 1130500
  7.2 52.7 %all-gather.2.cloned.1.call-start = ((), (), s32[]{:S(2)}) async-start(), calls=%async_computation.2 | async-start | bytes 2621440 | tf_op jit(solution)/shard_map/all_gather | solution.py:36
  7.2 67.4 %copy-start.1 = (bf16[184,4096]{1,0:T(8,128)(2,1)S(1)}, bf16[184,4096]{1,0:T(8,128)(2,1)}, u32[]{:S(2)}) copy-start(bf16[184,4096]{1,0:T(8,128)(2,1)} %param.7) | copy-start | bytes 4521988
  7.9 153.5 %reduce-scatter.5.cloned.1.call-start = ((), (), s32[]{:S(2)}) async-start(), calls=%async_computation.4 | async-start | bytes 655360 | tf_op jit(solution)/shard_map/reduce_scatter | solution.py:39
  27.2 38.1 %collective-permute-start.1 = (bf16[256,1024]{1,0:T(8,128)(2,1)S(1)}, bf16[256,1024]{1,0:T(8,128)(2,1)S(1)}, u32[]{:S(2)}, u32[]{:S(2)}) collective-permute-start(bf16[256,1024]{1,0:T(8,128)(2,1)S(1)} %all_gather.7), channel_id=1, source_target_pairs={{0,1},{1,0},{2,3},{3,2},{4,5},{5,4},{6,7},{7,6},{8,9},{9,8},{10,11... | collective-permute-start | bytes 1572872 | tf_op jit(solution)/shard_map/ppermute | solution.py:44
  27.2 48.1 %collective-permute-start.3 = (bf16[184,4096]{1,0:T(8,128)(2,1)}, bf16[184,4096]{1,0:T(8,128)(2,1)}, u32[]{:S(2)}, u32[]{:S(2)}) collective-permute-start(bf16[184,4096]{1,0:T(8,128)(2,1)} %param.7), channel_id=1, source_target_pairs={{0,2},{1,3},{2,0},{3,1},{4,6},{5,7},{6,4},{7,5},{8,10},{9,11},{10,... | collective-permute-start | bytes 4521992 | tf_op jit(solution)/shard_map/ppermute | solution.py:47
  59.9 20.1 %collective-permute-start = (bf16[256,4096]{1,0:T(8,128)(2,1)}, bf16[256,4096]{1,0:T(8,128)(2,1)}, u32[]{:S(2)}, u32[]{:S(2)}) collective-permute-start(bf16[256,4096]{1,0:T(8,128)(2,1)} %all-gather.2.cloned.1.call-done), channel_id=1, source_target_pairs={{0,1},{1,0},{2,3},{3,2},{4,5},{5,4},{6,7},{7,6},{8,9},{9,8},{10,11... | collective-permute-start | bytes 6291464 | tf_op jit(solution)/shard_map/ppermute | solution.py:44
  61.2 4.4 %collective-permute-start.2 = (s32[184,1]{0,1:T(1,128)S(1)}, s32[184,1]{0,1:T(1,128)S(1)}, u32[]{:S(2)}, u32[]{:S(2)}) collective-permute-start(s32[184,1]{0,1:T(1,128)S(1)} %bitcast.67), channel_id=1, source_target_pairs={{0,2},{1,3},{2,0},{3,1},{4,6},{5,7},{6,4},{7,5},{8,10},{9,11},{10,... | collective-permute-start | bytes 2216 | tf_op jit(solution)/shard_map/ppermute | solution.py:47
  62.7 11.1 %collective-permute-start.5 = (bf16[184,1024]{1,0:T(8,128)(2,1)}, bf16[184,1024]{1,0:T(8,128)(2,1)S(1)}, u32[]{:S(2)}, u32[]{:S(2)}) collective-permute-start(bf16[184,1024]{1,0:T(8,128)(2,1)} %param.8), channel_id=1, source_target_pairs={{0,2},{1,3},{2,0},{3,1},{4,6},{5,7},{6,4},{7,5},{8,10},{9,11},{10,... | collective-permute-start | bytes 1130504 | tf_op jit(solution)/shard_map/ppermute | solution.py:47
  65.6 8.6 %copy-start.21 = (bf16[184,256]{1,0:T(8,128)(2,1)}, bf16[184,256]{1,0:T(8,128)(2,1)S(1)}, u32[]{:S(2)}) copy-start(bf16[184,256]{1,0:T(8,128)(2,1)S(1)} %fusion.27) | copy-start | bytes 282628
  75.3 3.8 %copy-start = (bf16[256,4096]{1,0:T(8,128)(2,1)S(1)}, bf16[256,4096]{1,0:T(8,128)(2,1)}, u32[]{:S(2)}) copy-start(bf16[256,4096]{1,0:T(8,128)(2,1)} %all-gather.2.cloned.1.call-done) | copy-start | bytes 6291460
  79.1 15.5 %collective-permute-start.7 = (bf16[256,4096]{1,0:T(8,128)(2,1)}, bf16[256,4096]{1,0:T(8,128)(2,1)}, u32[]{:S(2)}, u32[]{:S(2)}) collective-permute-start(bf16[256,4096]{1,0:T(8,128)(2,1)} %fusion.2), channel_id=1, source_target_pairs={{0,1},{1,0},{2,3},{3,2},{4,5},{5,4},{6,7},{7,6},{8,9},{9,8},{10,11... | collective-permute-start | bytes 6291464 | tf_op jit(solution)/shard_map/ppermute | solution.py:44
  80.0 7.4 %copy-start.16 = (bf16[184,256]{1,0:T(8,128)(2,1)}, bf16[184,256]{1,0:T(8,128)(2,1)S(1)}, u32[]{:S(2)}) copy-start(bf16[184,256]{1,0:T(8,128)(2,1)S(1)} %fusion.22) | copy-start | bytes 282628
  86.8 3.2 %collective-permute-start.8 = (bf16[256,1024]{1,0:T(8,128)(2,1)S(1)}, bf16[256,1024]{1,0:T(8,128)(2,1)S(1)}, u32[]{:S(2)}, u32[]{:S(2)}) collective-permute-start(bf16[256,1024]{1,0:T(8,128)(2,1)S(1)} %fusion.13), channel_id=1, source_target_pairs={{0,1},{1,0},{2,3},{3,2},{4,5},{5,4},{6,7},{7,6},{8,9},{9,8},{10,11... | collective-permute-start | bytes 1572872 | tf_op jit(solution)/shard_map/ppermute | solution.py:44
  91.7 71.2 %reduce-scatter.3.cloned.1.call-start = ((), (), s32[]{:S(2)}) async-start(), calls=%async_computation.3 | async-start | bytes 2621440 | tf_op jit(solution)/shard_map/reduce_scatter | solution.py:39
  99.6 8.0 %copy-start.3 = (bf16[184,4096]{1,0:T(8,128)(2,1)S(1)}, bf16[184,4096]{1,0:T(8,128)(2,1)}, u32[]{:S(2)}) copy-start(bf16[184,4096]{1,0:T(8,128)(2,1)} %param.7) | copy-start | bytes 4521988
  107.6 5.2 %copy-start.20 = (bf16[184,256]{1,0:T(8,128)(2,1)S(1)}, bf16[184,256]{1,0:T(8,128)(2,1)}, u32[]{:S(2)}) copy-start(bf16[184,256]{1,0:T(8,128)(2,1)} %copy-done.19) | copy-start | bytes 282628
  113.7 3.9 %copy-start.15 = (bf16[184,256]{1,0:T(8,128)(2,1)S(1)}, bf16[184,256]{1,0:T(8,128)(2,1)}, u32[]{:S(2)}) copy-start(bf16[184,256]{1,0:T(8,128)(2,1)} %copy-done.14) | copy-start | bytes 282628
  113.7 4.1 %copy-start.13 = (bf16[184,256]{1,0:T(8,128)(2,1)S(1)}, bf16[184,256]{1,0:T(8,128)(2,1)}, u32[]{:S(2)}) copy-start(bf16[184,256]{1,0:T(8,128)(2,1)} %copy-done.12) | copy-start | bytes 282628
  117.1 49.1 %collective-permute-start.6 = (bf16[184,4096]{1,0:T(8,128)(2,1)}, bf16[184,4096]{1,0:T(8,128)(2,1)}, u32[]{:S(2)}, u32[]{:S(2)}) collective-permute-start(bf16[184,4096]{1,0:T(8,128)(2,1)} %fusion.5), channel_id=1, source_target_pairs={{0,2},{1,3},{2,0},{3,1},{4,6},{5,7},{6,4},{7,5},{8,10},{9,11},{10,... | collective-permute-start | bytes 4521992 | tf_op jit(solution)/shard_map/ppermute | solution.py:47
  118.1 42.2 %collective-permute-start.4 = (bf16[184,1024]{1,0:T(8,128)(2,1)S(1)}, bf16[184,1024]{1,0:T(8,128)(2,1)S(1)}, u32[]{:S(2)}, u32[]{:S(2)}) collective-permute-start(bf16[184,1024]{1,0:T(8,128)(2,1)S(1)} %fusion.21), channel_id=1, source_target_pairs={{0,2},{1,3},{2,0},{3,1},{4,6},{5,7},{6,4},{7,5},{8,10},{9,11},{10,... | collective-permute-start | bytes 1130504 | tf_op jit(solution)/shard_map/ppermute | solution.py:47
  120.0 40.3 %copy-start.11 = (bf16[184,256]{1,0:T(8,128)(2,1)S(1)}, bf16[184,256]{1,0:T(8,128)(2,1)}, u32[]{:S(2)}) copy-start(bf16[184,256]{1,0:T(8,128)(2,1)} %copy-done.10) | copy-start | bytes 282628
  122.2 44.0 %copy-start.4 = (f32[184,4096]{1,0:T(8,128)S(1)}, f32[184,4096]{1,0:T(8,128)}, u32[]{:S(2)}) copy-start(f32[184,4096]{1,0:T(8,128)} %fusion.46) | copy-start | bytes 9043972
  166.2 38.3 %copy-start.6 = (bf16[64,4096]{1,0:T(8,128)(2,1)S(1)}, bf16[64,4096]{1,0:T(8,128)(2,1)}, u32[]{:S(2)}) copy-start(bf16[64,4096]{1,0:T(8,128)(2,1)} %reduce-scatter.3.cloned.1.call-done) | copy-start | bytes 1572868
  (12 other events, 22.4 us)
Sparse Core Ops, SparseCore 0:
  9.6 50.2 all-gather.1
  91.9 20.6 reduce-scatter.4
  114.8 42.1 reduce-scatter.2

commit v2 on v1

--- a/solution.py
+++ b/solution.py
@@ -1,6 +1,10 @@
+import functools
+
 import jax
 import jax.numpy as jnp
 from jax import lax
+from jax.experimental import pallas as pl
+from jax.experimental.pallas import tpu as pltpu
 from jax.sharding import PartitionSpec as P
 
 adapter_scale = 2.0
@@ -21,7 +25,7 @@
     return lax.dot_general(a, b, (((0,), (0,)), ((), ())), preferred_element_type=f32)
 
 
-def local(x, dy, w, down_f, up_f, owner, slot):
+def long_line(x, dy, w, down_f, up_f, owner, slot):
     n = lax.axis_size("dev")
     me = lax.axis_index("dev")
     layers = n // plane
@@ -99,6 +103,388 @@
     return (layer_out, grad_tokens, grad_a, grad_b)
 
 
+def copy_to(src, dst, send_sem, recv_sem, device):
+    return pltpu.make_async_remote_copy(
+        src_ref=src,
+        dst_ref=dst,
+        send_sem=send_sem,
+        recv_sem=recv_sem,
+        device_id={"dev": device},
+        device_id_type=pl.DeviceIdType.MESH,
+    )
+
+
+def greet(barrier, device):
+    pl.semaphore_signal(
+        barrier, inc=1, device_id={"dev": device}, device_id_type=pl.DeviceIdType.MESH
+    )
+
+
+def position():
+    me = lax.axis_index("dev")
+    z, core = me // plane, me % 2
+    return me, z, core, me + 1 - 2 * core
+
+
+def gather_kernel(layers, down, up, down_all, up_all, own_sem, send, recv, core_send, core_recv):
+    me, z, core, twin = position()
+    steps = layers - 1
+    arrays = ((down, down_all), (up, up_all))
+    inner = z > 0
+    outer = z < layers - 1
+    barrier = pltpu.get_barrier_semaphore()
+    greet(barrier, twin)
+    pl.when(inner)(lambda: greet(barrier, me - plane))
+    pl.when(outer)(lambda: greet(barrier, me + plane))
+    pl.semaphore_wait(barrier, 1 + inner.astype(jnp.int32) + outer.astype(jnp.int32))
+
+    def hop(way, s, a):
+        block = z - s if way == 0 else z + s
+        own, whole = arrays[a]
+        spot = whole.at[block, core]
+        k = (way * steps + s) * 2 + a
+        target = me + plane if way == 0 else me - plane
+        return copy_to(own if s == 0 else spot, spot, send.at[k], recv.at[k], target)
+
+    def landed(way, s, a):
+        block = z - 1 - s if way == 0 else z + 1 + s
+        own, whole = arrays[a]
+        k = (way * steps + s) * 2 + a
+        return copy_to(own, whole.at[block, core], send.at[k], recv.at[k], twin)
+
+    def across(way, s, a):
+        block = z - 1 - s if way == 0 else z + 1 + s
+        spot = arrays[a][1].at[block, core]
+        k = (way * steps + s) * 2 + a
+        return copy_to(spot, spot, core_send.at[k], core_recv.at[k], twin)
+
+    def from_twin(way, s, a):
+        block = z - 1 - s if way == 0 else z + 1 + s
+        spot = arrays[a][1].at[block, 1 - core]
+        k = (way * steps + s) * 2 + a
+        return copy_to(spot, spot, core_send.at[k], core_recv.at[k], twin)
+
+    def sends(way, s):
+        return (z >= s) & outer if way == 0 else (z + s <= layers - 1) & inner
+
+    def arrives(way, s):
+        return z - 1 - s >= 0 if way == 0 else z + 1 + s <= layers - 1
+
+    def each(copies, act):
+        def run():
+            for a in range(2):
+                act(copies(a))
+
+        return run
+
+    def start(c):
+        c.start()
+
+    base = 4 * steps
+
+    def own_across(a):
+        return copy_to(
+            arrays[a][0],
+            arrays[a][1].at[z, core],
+            core_send.at[base + a],
+            core_recv.at[base + a],
+            twin,
+        )
+
+    def own_from(a):
+        return copy_to(
+            arrays[a][0],
+            arrays[a][1].at[z, 1 - core],
+            core_send.at[base + a],
+            core_recv.at[base + a],
+            twin,
+        )
+
+    def own_copy(a):
+        return pltpu.make_async_copy(arrays[a][0], arrays[a][1].at[z, core], own_sem.at[a])
+
+    for s in range(steps):
+        for way in range(2):
+            pl.when(sends(way, s))(each(functools.partial(hop, way, s), start))
+        if s == 0:
+            each(own_across, start)()
+            each(own_copy, start)()
+        for way in range(2):
+            pl.when(arrives(way, s))(
+                each(functools.partial(landed, way, s), lambda c: c.wait_recv())
+            )
+        for way in range(2):
+            pl.when(arrives(way, s))(each(functools.partial(across, way, s), start))
+    for a in range(2):
+        own_copy(a).wait()
+        own_across(a).wait_send()
+        own_from(a).wait_recv()
+    for s in range(steps):
+        for way in range(2):
+            pl.when(sends(way, s))(each(functools.partial(hop, way, s), lambda c: c.wait_send()))
+            pl.when(arrives(way, s))(
+                each(functools.partial(across, way, s), lambda c: c.wait_send())
+            )
+            pl.when(arrives(way, s))(
+                each(functools.partial(from_twin, way, s), lambda c: c.wait_recv())
+            )
+
+
+def reduce_kernel(
+    layers,
+    rounds,
+    limit,
+    part_a,
+    part_b,
+    out_a,
+    out_b,
+    twin_a,
+    twin_b,
+    sum_a,
+    sum_b,
+    in_a,
+    in_b,
+    send_a,
+    send_b,
+    norm_buf,
+    twin_send,
+    twin_recv,
+    hop_send,
+    hop_recv,
+    norm_send,
+    norm_recv,
+):
+    me, z, core, twin = position()
+    inner = z > 0
+    outer = z < layers - 1
+    arrays = (
+        (part_a, twin_a, sum_a, in_a, send_a),
+        (part_b, twin_b, sum_b, in_b, send_b),
+    )
+    partners = []
+    for r in range(rounds):
+        bit = 2**r
+        partners.append(me + bit - 2 * bit * ((me // bit) % 2))
+    barrier = pltpu.get_barrier_semaphore()
+    for p in partners:
+        greet(barrier, p)
+    pl.when(inner)(lambda: greet(barrier, me - plane))
+    pl.when(outer)(lambda: greet(barrier, me + plane))
+    pl.semaphore_wait(barrier, rounds + inner.astype(jnp.int32) + outer.astype(jnp.int32))
+
+    order = []
+    for i in range((layers + 1) // 2):
+        order += [layers - 1 - i, i] if layers - 1 - i != i else [i]
+
+    def to_twin(j, a):
+        part, got = arrays[a][:2]
+        k = 2 * j + a
+        return copy_to(part.at[j, 1 - core], got.at[j], twin_send.at[k], twin_recv.at[k], twin)
+
+    for j in order:
+        for a in range(2):
+            to_twin(j, a).start()
+
+    ready = set()
+
+    def prepare(j):
+        if j in ready:
+            return
+        ready.add(j)
+        for a in range(2):
+            part, got, total = arrays[a][:3]
+            to_twin(j, a).wait_recv()
+            total[j] = part[j, core].astype(f32) + got[j].astype(f32)
+
+    def hop(way, j, a):
+        k = (way * layers + j) * 2 + a
+        return copy_to(
+            arrays[a][4].at[way, j],
+            arrays[a][3].at[way, j],
+            hop_send.at[k],
+            hop_recv.at[k],
+            me + plane if way == 0 else me - plane,
+        )
+
+    def take(way, j):
+        for a in range(2):
+            total, came = arrays[a][2:4]
+            hop(way, j, a).wait_recv()
+            total[j] = total[j] + came[way, j].astype(f32)
+
+    def forward(way, j):
+        pl.when(inner if way == 0 else outer)(lambda: take(way, j))
+        for a in range(2):
+            total, _, out = arrays[a][2:]
+            out[way, j] = total[j].astype(bf16)
+            hop(way, j, a).start()
+
+    def moves(way, j):
+        return z < j if way == 0 else z > j
+
+    for i in range(layers - 1):
+        for way, j in ((0, layers - 1 - i), (1, i)):
+            prepare(j)
+            pl.when(moves(way, j))(functools.partial(forward, way, j))
+    for j in range(layers):
+        prepare(j)
+    for j in range(layers):
+        if j > 0:
+            pl.when(z == j)(functools.partial(take, 0, j))
+        if j < layers - 1:
+            pl.when(z == j)(functools.partial(take, 1, j))
+
+    raw_a = sum_a[z] * adapter_scale
+    raw_b = sum_b[z] * adapter_scale
+    squares = jnp.sum(raw_a * raw_a) + jnp.sum(raw_b * raw_b)
+    norm_buf[0] = jnp.full(norm_buf.shape[1:], squares, f32)
+    for r, p in enumerate(partners):
+        c = copy_to(norm_buf.at[2 * r], norm_buf.at[2 * r + 1], norm_send.at[r], norm_recv.at[r], p)
+        c.start()
+        c.wait()
+        norm_buf[2 * r + 2] = norm_buf[2 * r] + norm_buf[2 * r + 1]
+    norm = jnp.sqrt(norm_buf[2 * rounds][0:1, 0:1])
+    factor = jnp.minimum(f32(1.0), f32(limit) / (norm + f32(1e-06)))
+    out_a[...] = (sum_a[z] * adapter_scale * factor).astype(bf16)
+    out_b[...] = (sum_b[z] * adapter_scale * factor).astype(bf16)
+
+    for j in range(layers):
+        for a in range(2):
+            to_twin(j, a).wait_send()
+        for way in range(2):
+            if (way == 0 and j > 0) or (way == 1 and j < layers - 1):
+
+                def settle(way=way, j=j):
+                    for a in range(2):
+                        hop(way, j, a).wait_send()
+
+                pl.when(moves(way, j))(settle)
+
+
+def gather_line(layers, down, up):
+    cols, hidden = down.shape
+    width = up.shape[1]
+    sems = 4 * (layers - 1)
+    return pl.pallas_call(
+        functools.partial(gather_kernel, layers),
+        out_shape=(
+            jax.ShapeDtypeStruct((layers, 2, cols, hidden), bf16),
+            jax.ShapeDtypeStruct((layers, 2, cols, width), bf16),
+        ),
+        in_specs=[pl.BlockSpec(memory_space=pl.ANY)] * 2,
+        out_specs=[pl.BlockSpec(memory_space=pl.ANY)] * 2,
+        scratch_shapes=[
+            pltpu.SemaphoreType.DMA((2,)),
+            pltpu.SemaphoreType.DMA((sems,)),
+            pltpu.SemaphoreType.DMA((sems,)),
+            pltpu.SemaphoreType.DMA((sems + 2,)),
+            pltpu.SemaphoreType.DMA((sems + 2,)),
+        ],
+        cost_estimate=pl.CostEstimate(flops=0, bytes_accessed=100_000_000, transcendentals=0),
+        compiler_params=pltpu.CompilerParams(collective_id=0, has_side_effects=True),
+    )(down, up)
+
+
+def reduce_line(layers, n, limit, part_a, part_b):
+    _, _, cols, hidden = part_a.shape
+    width = part_b.shape[3]
+    rounds = n.bit_length() - 1
+    vmem = pl.BlockSpec(memory_space=pltpu.VMEM)
+
+    def both(lead, dtype):
+        return [pltpu.VMEM((*lead, cols, m), dtype) for m in (hidden, width)]
+
+    return pl.pallas_call(
+        functools.partial(reduce_kernel, layers, rounds, limit),
+        out_shape=(
+            jax.ShapeDtypeStruct((cols, hidden), bf16),
+            jax.ShapeDtypeStruct((cols, width), bf16),
+        ),
+        in_specs=[vmem] * 2,
+        out_specs=[vmem] * 2,
+        scratch_shapes=[
+            *both((layers,), bf16),
+            *both((layers,), f32),
+            *both((2, layers), bf16),
+            *both((2, layers), bf16),
+            pltpu.VMEM((2 * rounds + 1, 8, 128), f32),
+            pltpu.SemaphoreType.DMA((2 * layers,)),
+            pltpu.SemaphoreType.DMA((2 * layers,)),
+            pltpu.SemaphoreType.DMA((4 * layers,)),
+            pltpu.SemaphoreType.DMA((4 * layers,)),
+            pltpu.SemaphoreType.DMA((rounds,)),
+            pltpu.SemaphoreType.DMA((rounds,)),
+        ],
+        cost_estimate=pl.CostEstimate(flops=0, bytes_accessed=100_000_000, transcendentals=0),
+        compiler_params=pltpu.CompilerParams(
+            collective_id=1, has_side_effects=True, vmem_limit_bytes=48 * 2**20
+        ),
+    )(part_a, part_b)
+
+
+def short_line(x, dy, w, down_f, up_f, owner, slot):
+    n = lax.axis_size("dev")
+    me = lax.axis_index("dev")
+    layers = n // plane
+    tenants, hidden, rank = down_f.shape
+    width = up_f.shape[2]
+    cols = tenants * rank
+    to_line = [(i, i ^ 2) for i in range(n)]
+
+    def swap_line(v):
+        return lax.ppermute(v, "dev", to_line)
+
+    ids = (owner[:, 0] * tenants + slot).reshape(-1, 1)
+    ids_p = swap_line(ids)
+    dy_p = swap_line(dy)
+    x_p = swap_line(x)
+    downs, ups = gather_line(
+        layers,
+        jnp.transpose(down_f, (0, 2, 1)).reshape(cols, hidden),
+        up_f.reshape(cols, width),
+    )
+    downs = downs.reshape(layers * 2 * cols, hidden)
+    ups = ups.reshape(layers * 2 * cols, width)
+    frozen_y = dot_nn(x, w)
+    frozen_dx = dot_nt(dy, w)
+
+    col = jnp.arange(layers * 2 * cols, dtype=jnp.int32)[None, :]
+    device = (col // (2 * cols)) * plane + (me % plane) // 2 * 2 + (col // cols) % 2
+    label = device * tenants + (col // rank) % tenants
+
+    def masked(v, i):
+        return jnp.where(i == label, v, 0.0).astype(bf16)
+
+    back_p = masked(dot_nt(dy_p, ups), ids_p)
+    far_dx = swap_line((adapter_scale * dot_nn(back_p, downs)).astype(bf16))
+    proj_p = masked(dot_nt(x_p, downs), ids_p)
+    far_y = swap_line((adapter_scale * dot_nn(proj_p, ups)).astype(bf16))
+    back = masked(dot_nt(dy, ups), ids)
+    proj = masked(dot_nt(x, downs), ids)
+    part_a = (dot_tn(back, x) + dot_tn(back_p, x_p)).astype(bf16)
+    part_b = (dot_tn(proj, dy) + dot_tn(proj_p, dy_p)).astype(bf16)
+    near_dx = (adapter_scale * dot_nn(back, downs)).astype(bf16)
+    near_y = (adapter_scale * dot_nn(proj, ups)).astype(bf16)
+    limit = float(tenants * n * rank * (hidden + width)) ** 0.5
+    grad_a, grad_b = reduce_line(
+        layers,
+        n,
+        limit,
+        part_a.reshape(layers, 2, cols, hidden),
+        part_b.reshape(layers, 2, cols, width),
+    )
+    layer_out = (frozen_y + (near_y.astype(f32) + far_y.astype(f32))).astype(bf16)
+    grad_tokens = (frozen_dx + (near_dx.astype(f32) + far_dx.astype(f32))).astype(bf16)
+    grad_a = jnp.transpose(grad_a.reshape(tenants, rank, hidden), (0, 2, 1))
+    return (layer_out, grad_tokens, grad_a, grad_b.reshape(tenants, rank, width))
+
+
+def local(*args):
+    if lax.axis_size("dev") // plane <= 4:
+        return short_line(*args)
+    return long_line(*args)
+
+
 def solution(mesh):
     rows = P(("groups", "dev"), None)
     stack = P(("groups", "dev"), None, None)

time: 212 us -> 172 us (0.81)
  Pallas kernels: 0 us -> 129 us
  waiting for transfers between devices: 78.1 us -> 0.01 us
  blocking collectives: 50.2 us -> 0 us
  matrix products: 50.9 us -> 32.3 us
  between operations: 16.2 us -> 0.8 us
  other arithmetic: 7.34 us -> 1.37 us
    pallas_call x0 -> x2, Pallas kernels: none -> 129 us  [the longest x1 76.6 us: reduce_line(): pl.pallas_call(functools.partial(reduce_kernel, layers, rounds, limit), o...]
    ppermute x5, waiting for transfers between devices: 46.3 us -> 0.01 us  [swap_line(): return lax.ppermute(v, 'dev', to_line)]
    all_gather x1 -> x0, waiting for transfers between devices: 31.1 us -> none  [gather(): return lax.all_gather(v, 'dev', axis_index_groups=columns, tiled=True)]
    psum x1 -> x0, blocking collectives: 31 us -> none  [local(): norm = jnp.sqrt(lax.psum(jnp.sum(ga * ga) + jnp.sum(gb * gb), 'dev'))]
    all_gather x1 -> x0, blocking collectives: 19.2 us -> none  [gather(): return lax.all_gather(v, 'dev', axis_index_groups=columns, tiled=True)]
    dot_general x9 -> x5, matrix products: 19.5 us -> 10.6 us  [dot_nt(): lax.dot_general(a, b, (((1,), (1,)), ((), ())), preferred_element_type=f32)]
    dot_general x8 -> x4, matrix products: 13.2 us -> 7.55 us  [dot_tn(): lax.dot_general(a, b, (((0,), (0,)), ((), ())), preferred_element_type=f32)]
    dot_general x9 -> x5, matrix products: 18.1 us -> 14.2 us  [dot_nn(): lax.dot_general(a, b, (((1,), (0,)), ((), ())), preferred_element_type=f32)]
  transfers between devices with their start and end apart: 12 -> 5, of which waited for: 3 -> 0; matrix products, arithmetic and copies ran while one was open for 24% -> 18% of each run, Pallas kernels for 0% -> 75%
where the time goes in v2:
time: 172 us
  Pallas kernels  129 us (75%)
  matrix products  32.3 us (19%)
  starting transfers between devices  7.1 us (4%)
    pallas_call x1, Pallas kernels, reduce_line(): pl.pallas_call(functools.partial(reduce_kernel, layers, rounds, limit), o...  76.6 us
    pallas_call x1, Pallas kernels, gather_line(): pl.pallas_call(functools.partial(gather_kernel, layers), out_shape=(jax.S...  51.9 us
    dot_general x5, matrix products, dot_nn(): lax.dot_general(a, b, (((1,), (0,)), ((), ())), preferred_element_type=f32)  14.2 us
    dot_general x5, matrix products, dot_nt(): lax.dot_general(a, b, (((1,), (1,)), ((), ())), preferred_element_type=f32)  10.6 us
    dot_general x4, matrix products, dot_tn(): lax.dot_general(a, b, (((0,), (0,)), ((), ())), preferred_element_type=f32)  7.55 us
    ppermute x5, starting transfers between devices, swap_line(): return lax.ppermute(v, 'dev', to_line)  7.1 us
  transfers between devices with their start and end apart: 5, of which 0 were waited for; matrix products, arithmetic and copies ran while one was open for 18% of the time, Pallas kernels for 75%

profile of v2, /device:TPU:0, one launch (start us, length us, event | category | flops | bytes accessed | tf_op | source)
XLA Modules:
  0.0 171.8 jit_solution(8708878073140740902)
XLA Ops:
  0.6 3.0 %collective-permute-start.1 = (bf16[184,4096]{1,0:T(8,128)(2,1)}, bf16[184,4096]{1,0:T(8,128)(2,1)}, u32[]{:S(2)}, u32[]{:S(2)}) collective-permute-start(bf16[184,4096]{1,0:T(8,128)(2,1)} %param.7), channel_id=1, source_target_pairs={{0,2},{1,3},{2,0},{3,1},{4,6},{5,7},{6,4},{7,5},{8,10},{9,11},{10,... | collective-permute-start | bytes 4521992 | tf_op jit(solution)/shard_map/ppermute | solution.py:435
  3.7 0.7 broadcast_multiply_fusion
  4.3 0.7 add.91
  5.0 2.0 %collective-permute-start.3 = (bf16[184,1024]{1,0:T(8,128)(2,1)}, bf16[184,1024]{1,0:T(8,128)(2,1)}, u32[]{:S(2)}, u32[]{:S(2)}) collective-permute-start(bf16[184,1024]{1,0:T(8,128)(2,1)} %param.8), channel_id=1, source_target_pairs={{0,2},{1,3},{2,0},{3,1},{4,6},{5,7},{6,4},{7,5},{8,10},{9,11},{10,... | collective-permute-start | bytes 1130504 | tf_op jit(solution)/shard_map/ppermute | solution.py:435
  7.1 6.6 %fusion.28 = f32[184,1024]{1,0:T(8,128)} fusion(bf16[184,4096]{1,0:T(8,128)(2,1)} %param.7, bf16[4096,1024]{1,0:T(8,128)(2,1)} %param.9), kind=kOutput, calls=%fused_computation.57 | convolution fusion | flops 1543503872 | bytes 10649600 | tf_op jit(solution)/shard_map/dot_general | solution.py:17
  13.6 2.9 %fusion.29 = f32[184,4096]{1,0:T(8,128)S(1)} fusion(bf16[184,1024]{1,0:T(8,128)(2,1)S(1)} %copy-done.3, bf16[4096,1024]{1,0:T(8,128)(2,1)S(1)} %copy-done.1), kind=kOutput, calls=%fused_computation.58 | convolution fusion | flops 1543503872 | bytes 11780096 | tf_op jit(solution)/shard_map/dot_general | solution.py:21
  16.5 51.9 %shard_map.102 = (bf16[4,2,64,4096]{3,2,1,0:T(8,128)(2,1)}, bf16[4,2,64,1024]{3,2,1,0:T(8,128)(2,1)}) custom-call(bf16[64,4096]{1,0:T(8,128)(2,1)} %bitcast.79, bf16[64,1024]{1,0:T(8,128)(2,1)} %bitcast.80), custom_call_target="tpu_custom_call" | custom-call | bytes 100000000 | tf_op jit(solution)/shard_map/pallas_call | solution.py:368
  68.5 1.7 %fusion.11 = bf16[184,512]{1,0:T(8,128)(2,1)S(1)} fusion(bf16[512,1024]{1,0:T(8,128)(2,1)} %bitcast.75, bf16[184,1024]{1,0:T(8,128)(2,1)S(1)} %copy-done.3, s32[512]{0:T(512)S(1)} %fusion.18, s32[184]{0:T(256)S(1)} %add.91), kind=kOutput, calls=%fused_computation.22 | convolution fusion | flops 193220608 | bytes 1616608 | tf_op jit(solution)/shard_map/dot_general | solution.py:21
  70.2 2.8 %fusion.30 = f32[512,4096]{1,0:T(8,128)S(1)} fusion(bf16[184,512]{1,0:T(8,128)(2,1)S(1)} %fusion.11, bf16[184,4096]{1,0:T(8,128)(2,1)} %param.7), kind=kOutput, calls=%fused_computation.59 | convolution fusion | flops 771751936 | bytes 10084352 | tf_op jit(solution)/shard_map/dot_general | solution.py:25
  73.3 1.5 fusion.13
  74.8 0.5 fusion.31
  75.3 1.5 fusion.10
  76.8 2.1 %fusion.2 = bf16[184,4096]{1,0:T(8,128)(2,1)} fusion(bf16[184,512]{1,0:T(8,128)(2,1)S(1)} %fusion.10, bf16[512,4096]{1,0:T(8,128)(2,1)S(1)} %bitcast.72), kind=kOutput, calls=%fused_computation.5 | convolution fusion | flops 773259264 | bytes 5890048 | tf_op jit(solution)/shard_map/dot_general | solution.py:17
  78.9 0.5 collective-permute-start.4
  79.4 2.9 %fusion.12 = bf16[184,512]{1,0:T(8,128)(2,1)S(1)} fusion(bf16[512,4096]{1,0:T(8,128)(2,1)S(1)} %bitcast.73, bf16[184,4096]{1,0:T(8,128)(2,1)} %collective-permute-done.1, s32[512]{0:T(512)S(1)} %fusion.18, s32[184]{0:T(256)S(1)} %bitcast.84), kind=kOutput, calls=%fused_computation.23 | convolution fusion | flops 772034560 | bytes 5892832 | tf_op jit(solution)/shard_map/dot_general | solution.py:21
  82.4 1.1 fusion.5
  83.5 1.5 collective-permute-start.2
  85.0 2.8 %add_convert_fusion = bf16[512,4096]{1,0:T(8,128)(2,1)S(1)} fusion(f32[512,4096]{1,0:T(8,128)S(1)} %fusion.30, bf16[184,512]{1,0:T(8,128)(2,1)S(1)} %fusion.10, bf16[184,4096]{1,0:T(8,128)(2,1)} %collective-permute-done.1), kind=kOutput, calls=%fused_computation | convolution fusion | flops 775946240 | bytes 14278656 | tf_op jit(solution)/shard_map/dot_general | solution.py:25
  87.8 1.5 add_convert_fusion.2
  89.3 76.6 %shard_map.103 = (bf16[64,4096]{1,0:T(8,128)(2,1)S(1)}, bf16[64,1024]{1,0:T(8,128)(2,1)S(1)}) custom-call(bf16[4,2,64,4096]{3,2,1,0:T(8,128)(2,1)S(1)} %bitcast.67, bf16[4,2,64,1024]{3,2,1,0:T(8,128)(2,1)S(1)} %bitcast.68), custom_call_target="tpu_custom_call" | custom-call | bytes 100000000 | tf_op jit(solution)/shard_map/pallas_call | solution.py:397
  165.9 2.2 %add_convert_fusion.3 = bf16[184,1024]{1,0:T(8,128)(2,1)} fusion(f32[184,1024]{1,0:T(8,128)S(1)} %copy-done.5, bf16[184,1024]{1,0:T(8,128)(2,1)} %collective-permute-done.2, bf16[184,512]{1,0:T(8,128)(2,1)} %copy-done.6, bf16[512,1024]{1,0:T(8,128)(2,1)S(1)} %bitcast.78), kind=kOutput, calls=%fused_computation.25 | convolution fusion | flops 194256896 | bytes 2744320 | tf_op jit(solution)/shard_map/dot_general | solution.py:17
  168.1 2.2 %add_convert_fusion.1 = bf16[184,4096]{1,0:T(8,128)(2,1)} fusion(f32[184,4096]{1,0:T(8,128)S(1)} %fusion.29, bf16[184,4096]{1,0:T(8,128)(2,1)S(1)} %collective-permute-done.4, bf16[184,512]{1,0:T(8,128)(2,1)S(1)} %fusion.11, bf16[512,4096]{1,0:T(8,128)(2,1)S(1)} %bitcast.74), kind=kOutput, calls=%fused_computation.6 | convolution fusion | flops 777027584 | bytes 10412032 | tf_op jit(solution)/shard_map/dot_general | solution.py:17
  170.3 0.8 copy.13
  171.1 0.7 copy.14
  (21 shorter events, 0.3 us)
Async XLA Ops:
  0.6 78.8 %collective-permute-start.1 = (bf16[184,4096]{1,0:T(8,128)(2,1)}, bf16[184,4096]{1,0:T(8,128)(2,1)}, u32[]{:S(2)}, u32[]{:S(2)}) collective-permute-start(bf16[184,4096]{1,0:T(8,128)(2,1)} %param.7), channel_id=1, source_target_pairs={{0,2},{1,3},{2,0},{3,1},{4,6},{5,7},{6,4},{7,5},{8,10},{9,11},{10,... | collective-permute-start | bytes 4521992 | tf_op jit(solution)/shard_map/ppermute | solution.py:435
  5.0 70.3 %collective-permute-start = (s32[184,1]{0,1:T(1,128)S(1)}, s32[184,1]{0,1:T(1,128)S(1)}, u32[]{:S(2)}, u32[]{:S(2)}) collective-permute-start(s32[184,1]{0,1:T(1,128)S(1)} %bitcast.82), channel_id=1, source_target_pairs={{0,2},{1,3},{2,0},{3,1},{4,6},{5,7},{6,4},{7,5},{8,10},{9,11},{10,... | collective-permute-start | bytes 2216 | tf_op jit(solution)/shard_map/ppermute | solution.py:435
  5.0 70.3 %collective-permute-start.3 = (bf16[184,1024]{1,0:T(8,128)(2,1)}, bf16[184,1024]{1,0:T(8,128)(2,1)}, u32[]{:S(2)}, u32[]{:S(2)}) collective-permute-start(bf16[184,1024]{1,0:T(8,128)(2,1)} %param.8), channel_id=1, source_target_pairs={{0,2},{1,3},{2,0},{3,1},{4,6},{5,7},{6,4},{7,5},{8,10},{9,11},{10,... | collective-permute-start | bytes 1130504 | tf_op jit(solution)/shard_map/ppermute | solution.py:435
  7.1 6.6 %copy-start.1 = (bf16[4096,1024]{1,0:T(8,128)(2,1)S(1)}, bf16[4096,1024]{1,0:T(8,128)(2,1)}, u32[]{:S(2)}) copy-start(bf16[4096,1024]{1,0:T(8,128)(2,1)} %param.9) | copy-start | bytes 25165828
  7.1 6.6 %copy-start.3 = (bf16[184,1024]{1,0:T(8,128)(2,1)S(1)}, bf16[184,1024]{1,0:T(8,128)(2,1)}, u32[]{:S(2)}) copy-start(bf16[184,1024]{1,0:T(8,128)(2,1)} %param.8) | copy-start | bytes 1130500
  70.2 2.9 %copy-start = (bf16[4,2,64,4096]{3,2,1,0:T(8,128)(2,1)S(1)}, bf16[4,2,64,4096]{3,2,1,0:T(8,128)(2,1)}, u32[]{:S(2)}) copy-start(bf16[4,2,64,4096]{3,2,1,0:T(8,128)(2,1)} %get-tuple-element.8) | copy-start | bytes 12582916
  70.2 3.1 %copy-start.4 = (bf16[184,4096]{1,0:T(8,128)(2,1)S(1)}, bf16[184,4096]{1,0:T(8,128)(2,1)}, u32[]{:S(2)}) copy-start(bf16[184,4096]{1,0:T(8,128)(2,1)} %param.7) | copy-start | bytes 4521988
  73.3 2.0 %copy-start.2 = (bf16[4,2,64,1024]{3,2,1,0:T(8,128)(2,1)S(1)}, bf16[4,2,64,1024]{3,2,1,0:T(8,128)(2,1)}, u32[]{:S(2)}) copy-start(bf16[4,2,64,1024]{3,2,1,0:T(8,128)(2,1)} %get-tuple-element.9) | copy-start | bytes 3145732
  74.8 8.6 %copy-start.6 = (bf16[184,512]{1,0:T(8,128)(2,1)}, bf16[184,512]{1,0:T(8,128)(2,1)S(1)}, u32[]{:S(2)}) copy-start(bf16[184,512]{1,0:T(8,128)(2,1)S(1)} %fusion.13) | copy-start | bytes 565252
  78.9 89.2 %collective-permute-start.4 = (bf16[184,4096]{1,0:T(8,128)(2,1)}, bf16[184,4096]{1,0:T(8,128)(2,1)S(1)}, u32[]{:S(2)}, u32[]{:S(2)}) collective-permute-start(bf16[184,4096]{1,0:T(8,128)(2,1)} %fusion.2), channel_id=1, source_target_pairs={{0,2},{1,3},{2,0},{3,1},{4,6},{5,7},{6,4},{7,5},{8,10},{9,11},{10,... | collective-permute-start | bytes 4521992 | tf_op jit(solution)/shard_map/ppermute | solution.py:435
  83.5 82.4 %collective-permute-start.2 = (bf16[184,1024]{1,0:T(8,128)(2,1)}, bf16[184,1024]{1,0:T(8,128)(2,1)}, u32[]{:S(2)}, u32[]{:S(2)}) collective-permute-start(bf16[184,1024]{1,0:T(8,128)(2,1)} %fusion.5), channel_id=1, source_target_pairs={{0,2},{1,3},{2,0},{3,1},{4,6},{5,7},{6,4},{7,5},{8,10},{9,11},{10,... | collective-permute-start | bytes 1130504 | tf_op jit(solution)/shard_map/ppermute | solution.py:435
  89.3 76.6 %copy-start.5 = (f32[184,1024]{1,0:T(8,128)S(1)}, f32[184,1024]{1,0:T(8,128)}, u32[]{:S(2)}) copy-start(f32[184,1024]{1,0:T(8,128)} %fusion.28) | copy-start | bytes 2260996

commit v3 on v2

--- a/solution.py
+++ b/solution.py
@@ -8,6 +8,7 @@
 from jax.sharding import PartitionSpec as P
 
 adapter_scale = 2.0
+piece = 512
 plane = 4
 f32 = jnp.float32
 bf16 = jnp.bfloat16
@@ -126,7 +127,27 @@
     return me, z, core, me + 1 - 2 * core
 
 
-def gather_kernel(layers, down, up, down_all, up_all, own_sem, send, recv, core_send, core_recv):
+def gather_kernel(
+    layers,
+    down,
+    up,
+    x,
+    dy,
+    w,
+    down_all,
+    up_all,
+    frozen_y,
+    frozen_dx,
+    w_vmem,
+    w_sem,
+    own_sem,
+    send,
+    recv,
+    core_send,
+    core_recv,
+):
+    load = pltpu.make_async_copy(w, w_vmem, w_sem)
+    load.start()
     me, z, core, twin = position()
     steps = layers - 1
     arrays = ((down, down_all), (up, up_all))
@@ -209,6 +230,17 @@
         if s == 0:
             each(own_across, start)()
             each(own_copy, start)()
+            load.wait()
+            frozen_y[...] = jnp.zeros_like(frozen_y)
+
+            def products(i, carry):
+                part = pl.ds(pl.multiple_of(i * piece, piece), piece)
+                block = w_vmem[part, :]
+                frozen_y[...] += dot_nn(x[:, part], block)
+                frozen_dx[:, part] = dot_nt(dy[...], block)
+                return carry
+
+            lax.fori_loop(0, w_vmem.shape[0] // piece, products, 0)
         for way in range(2):
             pl.when(arrives(way, s))(
                 each(functools.partial(landed, way, s), lambda c: c.wait_recv())
@@ -319,13 +351,18 @@
             out[way, j] = total[j].astype(bf16)
             hop(way, j, a).start()
 
+    lower = z < layers // 2
+
     def moves(way, j):
         return z < j if way == 0 else z > j
 
     for i in range(layers - 1):
-        for way, j in ((0, layers - 1 - i), (1, i)):
-            prepare(j)
-            pl.when(moves(way, j))(functools.partial(forward, way, j))
+        far, near = layers - 1 - i, i
+        prepare(far)
+        prepare(near)
+        pl.when(moves(0, far) & lower)(functools.partial(forward, 0, far))
+        pl.when(moves(1, near))(functools.partial(forward, 1, near))
+        pl.when(moves(0, far) & ~lower)(functools.partial(forward, 0, far))
     for j in range(layers):
         prepare(j)
     for j in range(layers):
@@ -361,19 +398,25 @@
                 pl.when(moves(way, j))(settle)
 
 
-def gather_line(layers, down, up):
+def gather_line(layers, down, up, x, dy, w):
     cols, hidden = down.shape
     width = up.shape[1]
     sems = 4 * (layers - 1)
+    anywhere = pl.BlockSpec(memory_space=pl.ANY)
+    vmem = pl.BlockSpec(memory_space=pltpu.VMEM)
     return pl.pallas_call(
         functools.partial(gather_kernel, layers),
         out_shape=(
             jax.ShapeDtypeStruct((layers, 2, cols, hidden), bf16),
             jax.ShapeDtypeStruct((layers, 2, cols, width), bf16),
+            jax.ShapeDtypeStruct(dy.shape, f32),
+            jax.ShapeDtypeStruct(x.shape, f32),
         ),
-        in_specs=[pl.BlockSpec(memory_space=pl.ANY)] * 2,
-        out_specs=[pl.BlockSpec(memory_space=pl.ANY)] * 2,
+        in_specs=[anywhere, anywhere, vmem, vmem, anywhere],
+        out_specs=[anywhere, anywhere, vmem, vmem],
         scratch_shapes=[
+            pltpu.VMEM(w.shape, bf16),
+            pltpu.SemaphoreType.DMA,
             pltpu.SemaphoreType.DMA((2,)),
             pltpu.SemaphoreType.DMA((sems,)),
             pltpu.SemaphoreType.DMA((sems,)),
@@ -381,8 +424,10 @@
             pltpu.SemaphoreType.DMA((sems + 2,)),
         ],
         cost_estimate=pl.CostEstimate(flops=0, bytes_accessed=100_000_000, transcendentals=0),
-        compiler_params=pltpu.CompilerParams(collective_id=0, has_side_effects=True),
-    )(down, up)
+        compiler_params=pltpu.CompilerParams(
+            collective_id=0, has_side_effects=True, vmem_limit_bytes=40 * 2**20
+        ),
+    )(down, up, x, dy, w)
 
 
 def reduce_line(layers, n, limit, part_a, part_b):
@@ -438,15 +483,16 @@
     ids_p = swap_line(ids)
     dy_p = swap_line(dy)
     x_p = swap_line(x)
-    downs, ups = gather_line(
+    downs, ups, frozen_y, frozen_dx = gather_line(
         layers,
         jnp.transpose(down_f, (0, 2, 1)).reshape(cols, hidden),
         up_f.reshape(cols, width),
+        x,
+        dy,
+        w,
     )
     downs = downs.reshape(layers * 2 * cols, hidden)
     ups = ups.reshape(layers * 2 * cols, width)
-    frozen_y = dot_nn(x, w)
-    frozen_dx = dot_nt(dy, w)
 
     col = jnp.arange(layers * 2 * cols, dtype=jnp.int32)[None, :]
     device = (col // (2 * cols)) * plane + (me % plane) // 2 * 2 + (col // cols) % 2

time: 172 us -> 147 us (0.85)
  Pallas kernels: 129 us -> 113 us
  matrix products: 32.3 us -> 18.1 us
  local copies, waits for them, and re-layouts: 1.7 us -> 5.78 us
    pallas_call x1, Pallas kernels: 76.6 us -> 62.5 us  [reduce_line(): pl.pallas_call(functools.partial(reduce_kernel, layers, rounds, limit), o...]
    dot_general x5 -> x4, matrix products: 14.2 us -> 7.65 us  [dot_nn(): lax.dot_general(a, b, (((1,), (0,)), ((), ())), preferred_element_type=f32)]
    dot_general x5 -> x4, matrix products: 10.6 us -> 5.47 us  [dot_nt(): lax.dot_general(a, b, (((1,), (1,)), ((), ())), preferred_element_type=f32)]
    unnamed x16, local copies, waits for them, and re-layouts: 1.7 us -> 5.78 us
    dot_general x4, matrix products: 7.55 us -> 5.01 us  [dot_tn(): lax.dot_general(a, b, (((0,), (0,)), ((), ())), preferred_element_type=f32)]
  transfers between devices with their start and end apart: 5 -> 5, of which waited for: 0 -> 0; matrix products, arithmetic and copies ran while one was open for 18% -> 12% of each run, Pallas kernels for 75% -> 77%
where the time goes in v3:
time: 147 us; the launch traced here: 146 us
  Pallas kernels  113 us (77%)
  matrix products  18.1 us (12%)
  starting transfers between devices  7.1 us (5%)
  local copies, waits for them, and re-layouts  5.78 us (4%)
    pallas_call x1, Pallas kernels, reduce_line(): pl.pallas_call(functools.partial(reduce_kernel, layers, rounds, limit), o...  62.5 us
    pallas_call x1, Pallas kernels, gather_line(): pl.pallas_call(functools.partial(gather_kernel, layers), out_shape=(jax.S...  50.8 us
    dot_general x4, matrix products, dot_nn(): lax.dot_general(a, b, (((1,), (0,)), ((), ())), preferred_element_type=f32)  7.65 us
    ppermute x5, starting transfers between devices, swap_line(): return lax.ppermute(v, 'dev', to_line)  7.1 us
    unnamed x16, local copies, waits for them, and re-layouts  5.78 us
    dot_general x4, matrix products, dot_nt(): lax.dot_general(a, b, (((1,), (1,)), ((), ())), preferred_element_type=f32)  5.47 us
    dot_general x4, matrix products, dot_tn(): lax.dot_general(a, b, (((0,), (0,)), ((), ())), preferred_element_type=f32)  5.01 us
  transfers between devices with their start and end apart: 5, of which 0 were waited for; matrix products, arithmetic and copies ran while one was open for 12% of the time, Pallas kernels for 77%

profile of v3, /device:TPU:0, one launch (start us, length us, event | category | flops | bytes accessed | tf_op | source)
XLA Modules:
  0.0 146.4 jit_solution(6323612682016531820)
XLA Ops:
  0.6 3.0 %collective-permute-start.1 = (bf16[184,4096]{1,0:T(8,128)(2,1)}, bf16[184,4096]{1,0:T(8,128)(2,1)}, u32[]{:S(2)}, u32[]{:S(2)}) collective-permute-start(bf16[184,4096]{1,0:T(8,128)(2,1)} %x.1), channel_id=1, source_target_pairs={{0,2},{1,3},{2,0},{3,1},{4,6},{5,7},{6,4},{7,5},{8,10},{9,11},{10,... | collective-permute-start | bytes 4521992 | tf_op jit(solution)/shard_map/ppermute | solution.py:480
  3.7 0.7 broadcast_multiply_fusion
  4.3 0.7 add.91
  5.0 2.0 %collective-permute-start.3 = (bf16[184,1024]{1,0:T(8,128)(2,1)}, bf16[184,1024]{1,0:T(8,128)(2,1)S(1)}, u32[]{:S(2)}, u32[]{:S(2)}) collective-permute-start(bf16[184,1024]{1,0:T(8,128)(2,1)} %dy.1), channel_id=1, source_target_pairs={{0,2},{1,3},{2,0},{3,1},{4,6},{5,7},{6,4},{7,5},{8,10},{9,11},{10,... | collective-permute-start | bytes 1130504 | tf_op jit(solution)/shard_map/ppermute | solution.py:480
  7.1 1.4 copy-done
  8.4 1.0 copy-done.1
  9.4 1.0 copy-done.2
  10.5 0.9 copy-done.3
  11.4 50.8 %shard_map.102 = (bf16[4,2,64,4096]{3,2,1,0:T(8,128)(2,1)S(1)}, bf16[4,2,64,1024]{3,2,1,0:T(8,128)(2,1)S(1)}, f32[184,1024]{1,0:T(8,128)S(1)}, f32[184,4096]{1,0:T(8,128)S(1)}) custom-call(bf16[64,4096]{1,0:T(8,128)(2,1)S(1)} %bitcast.74, bf16[64,1024]{1,0:T(8,128)(2,1)S(1)} %bitcast.75, bf16[184,4096]{1,0:T(8,128)(2,1)S(1)} %copy-done, ...), custom_call_target="tpu_custom_call" | custom-call | bytes 100000000 | tf_op jit(solution)/shard_map/pallas_call | solution.py:407
  62.2 0.5 fusion.11
  62.7 1.3 fusion.28
  64.1 1.5 %fusion.13 = bf16[184,512]{1,0:T(8,128)(2,1)S(1)} fusion(bf16[512,4096]{1,0:T(8,128)(2,1)S(1)} %bitcast.63, bf16[184,4096]{1,0:T(8,128)(2,1)S(1)} %copy-done, s32[512]{0:T(512)S(1)} %fusion.18, s32[184]{0:T(256)S(1)} %add.91), kind=kOutput, calls=%fused_computation.24 | convolution fusion | flops 772034560 | bytes 5892832 | tf_op jit(solution)/shard_map/dot_general | solution.py:22
  66.1 0.5 fusion.10
  66.6 2.1 %fusion.2 = bf16[184,4096]{1,0:T(8,128)(2,1)} fusion(bf16[184,512]{1,0:T(8,128)(2,1)S(1)} %fusion.10, bf16[512,4096]{1,0:T(8,128)(2,1)S(1)} %bitcast.64), kind=kOutput, calls=%fused_computation.5 | convolution fusion | flops 773259264 | bytes 5890048 | tf_op jit(solution)/shard_map/dot_general | solution.py:18
  68.7 0.5 collective-permute-start.4
  69.2 2.9 %fusion.12 = bf16[184,512]{1,0:T(8,128)(2,1)S(1)} fusion(bf16[512,4096]{1,0:T(8,128)(2,1)S(1)} %bitcast.65, bf16[184,4096]{1,0:T(8,128)(2,1)} %collective-permute-done.1, s32[512]{0:T(512)S(1)} %fusion.18, s32[184]{0:T(256)S(1)} %bitcast.80), kind=kOutput, calls=%fused_computation.23 | convolution fusion | flops 772034560 | bytes 5892832 | tf_op jit(solution)/shard_map/dot_general | solution.py:22
  72.2 1.1 fusion.5
  73.3 1.5 %collective-permute-start.2 = (bf16[184,1024]{1,0:T(8,128)(2,1)}, bf16[184,1024]{1,0:T(8,128)(2,1)}, u32[]{:S(2)}, u32[]{:S(2)}) collective-permute-start(bf16[184,1024]{1,0:T(8,128)(2,1)} %fusion.5), channel_id=1, source_target_pairs={{0,2},{1,3},{2,0},{3,1},{4,6},{5,7},{6,4},{7,5},{8,10},{9,11},{10,... | collective-permute-start | bytes 1130504 | tf_op jit(solution)/shard_map/ppermute | solution.py:480
  74.8 2.8 %add_convert_fusion = bf16[512,4096]{1,0:T(8,128)(2,1)S(1)} fusion(f32[512,4096]{1,0:T(8,128)S(1)} %fusion.28, bf16[184,512]{1,0:T(8,128)(2,1)S(1)} %fusion.10, bf16[184,4096]{1,0:T(8,128)(2,1)} %collective-permute-done.1), kind=kOutput, calls=%fused_computation | convolution fusion | flops 775946240 | bytes 14278656 | tf_op jit(solution)/shard_map/dot_general | solution.py:26
  78.0 62.5 %shard_map.103 = (bf16[64,4096]{1,0:T(8,128)(2,1)S(1)}, bf16[64,1024]{1,0:T(8,128)(2,1)S(1)}) custom-call(bf16[4,2,64,4096]{3,2,1,0:T(8,128)(2,1)S(1)} %bitcast.67, bf16[4,2,64,1024]{3,2,1,0:T(8,128)(2,1)S(1)} %bitcast.68), custom_call_target="tpu_custom_call" | custom-call | bytes 100000000 | tf_op jit(solution)/shard_map/pallas_call | solution.py:442
  140.5 2.2 %add_convert_fusion.3 = bf16[184,1024]{1,0:T(8,128)(2,1)} fusion(f32[184,1024]{1,0:T(8,128)S(1)} %get-tuple-element.10, bf16[184,1024]{1,0:T(8,128)(2,1)} %collective-permute-done.2, bf16[184,512]{1,0:T(8,128)(2,1)} %copy-done.4, bf16[512,1024]{1,0:T(8,128)(2,1)S(1)} %bitcast.72), kind=kOutput, calls=%fused_computation.25 | convolution fusion | flops 194256896 | bytes 2744320 | tf_op jit(solution)/shard_map/dot_general | solution.py:18
  142.7 2.3 %add_convert_fusion.1 = bf16[184,4096]{1,0:T(8,128)(2,1)} fusion(f32[184,4096]{1,0:T(8,128)S(1)} %get-tuple-element.13, bf16[184,4096]{1,0:T(8,128)(2,1)S(1)} %collective-permute-done.4, bf16[184,512]{1,0:T(8,128)(2,1)S(1)} %fusion.11, bf16[512,4096]{1,0:T(8,128)(2,1)S(1)} %bitcast.66), kind=kOutput, calls=%fused_computation.6 | convolution fusion | flops 777027584 | bytes 10412032 | tf_op jit(solution)/shard_map/dot_general | solution.py:18
  145.0 0.8 copy.13
  145.8 0.7 copy.14
  (19 shorter events, 1.0 us)
Async XLA Ops:
  0.6 68.6 %collective-permute-start.1 = (bf16[184,4096]{1,0:T(8,128)(2,1)}, bf16[184,4096]{1,0:T(8,128)(2,1)}, u32[]{:S(2)}, u32[]{:S(2)}) collective-permute-start(bf16[184,4096]{1,0:T(8,128)(2,1)} %x.1), channel_id=1, source_target_pairs={{0,2},{1,3},{2,0},{3,1},{4,6},{5,7},{6,4},{7,5},{8,10},{9,11},{10,... | collective-permute-start | bytes 4521992 | tf_op jit(solution)/shard_map/ppermute | solution.py:480
  5.0 61.0 %collective-permute-start = (s32[184,1]{0,1:T(1,128)S(1)}, s32[184,1]{0,1:T(1,128)S(1)}, u32[]{:S(2)}, u32[]{:S(2)}) collective-permute-start(s32[184,1]{0,1:T(1,128)S(1)} %bitcast.78), channel_id=1, source_target_pairs={{0,2},{1,3},{2,0},{3,1},{4,6},{5,7},{6,4},{7,5},{8,10},{9,11},{10,... | collective-permute-start | bytes 2216 | tf_op jit(solution)/shard_map/ppermute | solution.py:480
  5.0 61.0 %collective-permute-start.3 = (bf16[184,1024]{1,0:T(8,128)(2,1)}, bf16[184,1024]{1,0:T(8,128)(2,1)S(1)}, u32[]{:S(2)}, u32[]{:S(2)}) collective-permute-start(bf16[184,1024]{1,0:T(8,128)(2,1)} %dy.1), channel_id=1, source_target_pairs={{0,2},{1,3},{2,0},{3,1},{4,6},{5,7},{6,4},{7,5},{8,10},{9,11},{10,... | collective-permute-start | bytes 1130504 | tf_op jit(solution)/shard_map/ppermute | solution.py:480
  7.1 1.4 copy-start
  8.4 1.0 copy-start.1
  9.4 1.0 copy-start.2
  10.5 0.9 copy-start.3
  65.6 3.1 %copy-start.4 = (bf16[184,512]{1,0:T(8,128)(2,1)}, bf16[184,512]{1,0:T(8,128)(2,1)S(1)}, u32[]{:S(2)}) copy-start(bf16[184,512]{1,0:T(8,128)(2,1)S(1)} %fusion.13) | copy-start | bytes 565252
  66.1 2.6 %copy-start.5 = (bf16[184,1024]{1,0:T(8,128)(2,1)}, bf16[184,1024]{1,0:T(8,128)(2,1)S(1)}, u32[]{:S(2)}) copy-start(bf16[184,1024]{1,0:T(8,128)(2,1)S(1)} %collective-permute-done.3) | copy-start | bytes 1130500
  68.7 74.0 %collective-permute-start.4 = (bf16[184,4096]{1,0:T(8,128)(2,1)}, bf16[184,4096]{1,0:T(8,128)(2,1)S(1)}, u32[]{:S(2)}, u32[]{:S(2)}) collective-permute-start(bf16[184,4096]{1,0:T(8,128)(2,1)} %fusion.2), channel_id=1, source_target_pairs={{0,2},{1,3},{2,0},{3,1},{4,6},{5,7},{6,4},{7,5},{8,10},{9,11},{10,... | collective-permute-start | bytes 4521992 | tf_op jit(solution)/shard_map/ppermute | solution.py:480
  73.3 4.3 %copy-start.6 = (bf16[184,1024]{1,0:T(8,128)(2,1)S(1)}, bf16[184,1024]{1,0:T(8,128)(2,1)}, u32[]{:S(2)}) copy-start(bf16[184,1024]{1,0:T(8,128)(2,1)} %copy-done.5) | copy-start | bytes 1130500
  73.3 67.2 %collective-permute-start.2 = (bf16[184,1024]{1,0:T(8,128)(2,1)}, bf16[184,1024]{1,0:T(8,128)(2,1)}, u32[]{:S(2)}, u32[]{:S(2)}) collective-permute-start(bf16[184,1024]{1,0:T(8,128)(2,1)} %fusion.5), channel_id=1, source_target_pairs={{0,2},{1,3},{2,0},{3,1},{4,6},{5,7},{6,4},{7,5},{8,10},{9,11},{10,... | collective-permute-start | bytes 1130504 | tf_op jit(solution)/shard_map/ppermute | solution.py:480

commit v4 on v3

--- a/solution.py
+++ b/solution.py
@@ -138,8 +138,12 @@
     up_all,
     frozen_y,
     frozen_dx,
+    x_line,
+    dy_line,
     w_vmem,
     w_sem,
+    line_send,
+    line_recv,
     own_sem,
     send,
     recv,
@@ -149,15 +153,21 @@
     load = pltpu.make_async_copy(w, w_vmem, w_sem)
     load.start()
     me, z, core, twin = position()
+    across_y = me + 2 - 4 * ((me // 2) % 2)
     steps = layers - 1
     arrays = ((down, down_all), (up, up_all))
     inner = z > 0
     outer = z < layers - 1
     barrier = pltpu.get_barrier_semaphore()
     greet(barrier, twin)
+    greet(barrier, across_y)
     pl.when(inner)(lambda: greet(barrier, me - plane))
     pl.when(outer)(lambda: greet(barrier, me + plane))
-    pl.semaphore_wait(barrier, 1 + inner.astype(jnp.int32) + outer.astype(jnp.int32))
+    pl.semaphore_wait(barrier, 2 + inner.astype(jnp.int32) + outer.astype(jnp.int32))
+    rows = [
+        copy_to(dy, dy_line, line_send.at[0], line_recv.at[0], across_y),
+        copy_to(x, x_line, line_send.at[1], line_recv.at[1], across_y),
+    ]
 
     def hop(way, s, a):
         block = z - s if way == 0 else z + s
@@ -228,6 +238,8 @@
         for way in range(2):
             pl.when(sends(way, s))(each(functools.partial(hop, way, s), start))
         if s == 0:
+            for c in rows:
+                c.start()
             each(own_across, start)()
             each(own_copy, start)()
             load.wait()
@@ -247,6 +259,8 @@
             )
         for way in range(2):
             pl.when(arrives(way, s))(each(functools.partial(across, way, s), start))
+    for c in rows:
+        c.wait()
     for a in range(2):
         own_copy(a).wait()
         own_across(a).wait_send()
@@ -264,7 +278,6 @@
 
 def reduce_kernel(
     layers,
-    rounds,
     limit,
     part_a,
     part_b,
@@ -293,16 +306,18 @@
         (part_a, twin_a, sum_a, in_a, send_a),
         (part_b, twin_b, sum_b, in_b, send_b),
     )
-    partners = []
-    for r in range(rounds):
-        bit = 2**r
-        partners.append(me + bit - 2 * bit * ((me // bit) % 2))
+    def in_plane(k):
+        return me - me % plane + (me % plane + k) % plane
+
+    def in_column(k):
+        return (z + k) % layers * plane + me % plane
+
     barrier = pltpu.get_barrier_semaphore()
-    for p in partners:
-        greet(barrier, p)
-    pl.when(inner)(lambda: greet(barrier, me - plane))
-    pl.when(outer)(lambda: greet(barrier, me + plane))
-    pl.semaphore_wait(barrier, rounds + inner.astype(jnp.int32) + outer.astype(jnp.int32))
+    for k in range(1, plane):
+        greet(barrier, in_plane(k))
+    for k in range(1, layers):
+        greet(barrier, in_column(k))
+    pl.semaphore_wait(barrier, plane + layers - 2)
 
     order = []
     for i in range((layers + 1) // 2):
@@ -375,12 +390,25 @@
     raw_b = sum_b[z] * adapter_scale
     squares = jnp.sum(raw_a * raw_a) + jnp.sum(raw_b * raw_b)
     norm_buf[0] = jnp.full(norm_buf.shape[1:], squares, f32)
-    for r, p in enumerate(partners):
-        c = copy_to(norm_buf.at[2 * r], norm_buf.at[2 * r + 1], norm_send.at[r], norm_recv.at[r], p)
-        c.start()
-        c.wait()
-        norm_buf[2 * r + 2] = norm_buf[2 * r] + norm_buf[2 * r + 1]
-    norm = jnp.sqrt(norm_buf[2 * rounds][0:1, 0:1])
+
+    def share(first, count, target):
+        copies = []
+        for k in range(1, count):
+            at = first + k
+            copies.append(
+                copy_to(
+                    norm_buf.at[first], norm_buf.at[at], norm_send.at[at], norm_recv.at[at], target(k)
+                )
+            )
+            copies[-1].start()
+        total = norm_buf[first]
+        for k, c in enumerate(copies):
+            c.wait()
+            total = total + norm_buf[first + 1 + k]
+        return total
+
+    norm_buf[plane] = share(0, plane, in_plane)
+    norm = jnp.sqrt(share(plane, layers, in_column)[0:1, 0:1])
     factor = jnp.minimum(f32(1.0), f32(limit) / (norm + f32(1e-06)))
     out_a[...] = (sum_a[z] * adapter_scale * factor).astype(bf16)
     out_b[...] = (sum_b[z] * adapter_scale * factor).astype(bf16)
@@ -411,12 +439,16 @@
             jax.ShapeDtypeStruct((layers, 2, cols, width), bf16),
             jax.ShapeDtypeStruct(dy.shape, f32),
             jax.ShapeDtypeStruct(x.shape, f32),
+            jax.ShapeDtypeStruct(x.shape, bf16),
+            jax.ShapeDtypeStruct(dy.shape, bf16),
         ),
         in_specs=[anywhere, anywhere, vmem, vmem, anywhere],
-        out_specs=[anywhere, anywhere, vmem, vmem],
+        out_specs=[anywhere, anywhere, vmem, vmem, anywhere, anywhere],
         scratch_shapes=[
             pltpu.VMEM(w.shape, bf16),
             pltpu.SemaphoreType.DMA,
+            pltpu.SemaphoreType.DMA((2,)),
+            pltpu.SemaphoreType.DMA((2,)),
             pltpu.SemaphoreType.DMA((2,)),
             pltpu.SemaphoreType.DMA((sems,)),
             pltpu.SemaphoreType.DMA((sems,)),
@@ -430,17 +462,16 @@
     )(down, up, x, dy, w)
 
 
-def reduce_line(layers, n, limit, part_a, part_b):
+def reduce_line(layers, limit, part_a, part_b):
     _, _, cols, hidden = part_a.shape
     width = part_b.shape[3]
-    rounds = n.bit_length() - 1
     vmem = pl.BlockSpec(memory_space=pltpu.VMEM)
 
     def both(lead, dtype):
         return [pltpu.VMEM((*lead, cols, m), dtype) for m in (hidden, width)]
 
     return pl.pallas_call(
-        functools.partial(reduce_kernel, layers, rounds, limit),
+        functools.partial(reduce_kernel, layers, limit),
         out_shape=(
             jax.ShapeDtypeStruct((cols, hidden), bf16),
             jax.ShapeDtypeStruct((cols, width), bf16),
@@ -452,13 +483,13 @@
             *both((layers,), f32),
             *both((2, layers), bf16),
             *both((2, layers), bf16),
-            pltpu.VMEM((2 * rounds + 1, 8, 128), f32),
+            pltpu.VMEM((plane + layers, 8, 128), f32),
             pltpu.SemaphoreType.DMA((2 * layers,)),
             pltpu.SemaphoreType.DMA((2 * layers,)),
             pltpu.SemaphoreType.DMA((4 * layers,)),
             pltpu.SemaphoreType.DMA((4 * layers,)),
-            pltpu.SemaphoreType.DMA((rounds,)),
-            pltpu.SemaphoreType.DMA((rounds,)),
+            pltpu.SemaphoreType.DMA((plane + layers,)),
+            pltpu.SemaphoreType.DMA((plane + layers,)),
         ],
         cost_estimate=pl.CostEstimate(flops=0, bytes_accessed=100_000_000, transcendentals=0),
         compiler_params=pltpu.CompilerParams(
@@ -481,9 +512,7 @@
 
     ids = (owner[:, 0] * tenants + slot).reshape(-1, 1)
     ids_p = swap_line(ids)
-    dy_p = swap_line(dy)
-    x_p = swap_line(x)
-    downs, ups, frozen_y, frozen_dx = gather_line(
+    downs, ups, frozen_y, frozen_dx, x_p, dy_p = gather_line(
         layers,
         jnp.transpose(down_f, (0, 2, 1)).reshape(cols, hidden),
         up_f.reshape(cols, width),
@@ -514,7 +543,6 @@
     limit = float(tenants * n * rank * (hidden + width)) ** 0.5
     grad_a, grad_b = reduce_line(
         layers,
-        n,
         limit,
         part_a.reshape(layers, 2, cols, hidden),
         part_b.reshape(layers, 2, cols, width),

time: 147 us -> 138 us (0.939)
  Pallas kernels: 113 us -> 110 us
  matrix products: 18.1 us -> 15.3 us
  starting transfers between devices: 7.1 us -> 5 us
    pallas_call x1, Pallas kernels: 62.5 us -> 59.4 us  [reduce_line(): pl.pallas_call(functools.partial(reduce_kernel, layers, limit), out_shape...]
    ppermute x5 -> x3, starting transfers between devices: 7.1 us -> 5 us  [swap_line(): return lax.ppermute(v, 'dev', to_line)]
    unnamed x16 -> x12, local copies, waits for them, and re-layouts: 5.78 us -> 5.77 us
  transfers between devices with their start and end apart: 5 -> 3, of which waited for: 0 -> 0; matrix products, arithmetic and copies ran while one was open for 12% -> 8% of each run, Pallas kernels for 77% -> 80%
where the time goes in v4:
time: 138 us
  Pallas kernels  110 us (80%)
  matrix products  15.3 us (11%)
  local copies, waits for them, and re-layouts  5.77 us (4%)
  starting transfers between devices  5 us (4%)
    pallas_call x1, Pallas kernels, reduce_line(): pl.pallas_call(functools.partial(reduce_kernel, layers, limit), out_shape...  59.4 us
    pallas_call x1, Pallas kernels, gather_line(): pl.pallas_call(functools.partial(gather_kernel, layers), out_shape=(jax.S...  50.5 us
    dot_general x4, matrix products, dot_nn(): lax.dot_general(a, b, (((1,), (0,)), ((), ())), preferred_element_type=f32)  7.65 us
    unnamed x12, local copies, waits for them, and re-layouts  5.77 us
    ppermute x3, starting transfers between devices, swap_line(): return lax.ppermute(v, 'dev', to_line)  5 us
    dot_general x4, matrix products, dot_nt(): lax.dot_general(a, b, (((1,), (1,)), ((), ())), preferred_element_type=f32)  4.09 us
    dot_general x4, matrix products, dot_tn(): lax.dot_general(a, b, (((0,), (0,)), ((), ())), preferred_element_type=f32)  3.6 us
  transfers between devices with their start and end apart: 3, of which 0 were waited for; matrix products, arithmetic and copies ran while one was open for 8% of the time, Pallas kernels for 80%

profile of v4, /device:TPU:0, one launch (start us, length us, event | category | flops | bytes accessed | tf_op | source)
XLA Modules:
  0.0 138.1 jit_solution(15839867334737901160)
XLA Ops:
  0.6 0.7 broadcast_multiply_fusion
  1.3 0.7 add.91
  2.0 3.0 %collective-permute-start = (s32[184,1]{0,1:T(1,128)S(1)}, s32[184,1]{0,1:T(1,128)S(1)}, u32[]{:S(2)}, u32[]{:S(2)}) collective-permute-start(s32[184,1]{0,1:T(1,128)S(1)} %bitcast.66), channel_id=1, source_target_pairs={{0,2},{1,3},{2,0},{3,1},{4,6},{5,7},{6,4},{7,5},{8,10},{9,11},{10,... | collective-permute-start | bytes 2216 | tf_op jit(solution)/shard_map/ppermute | solution.py:511
  5.0 1.4 %copy-done = bf16[184,4096]{1,0:T(8,128)(2,1)S(1)} copy-done((bf16[184,4096]{1,0:T(8,128)(2,1)S(1)}, bf16[184,4096]{1,0:T(8,128)(2,1)}, u32[]{:S(2)}) %copy-start) | copy-done | bytes 1507352
  6.4 1.0 copy-done.1
  7.3 1.0 copy-done.2
  8.4 0.9 copy-done.3
  9.3 50.5 %shard_map.102 = (bf16[4,2,64,4096]{3,2,1,0:T(8,128)(2,1)S(1)}, bf16[4,2,64,1024]{3,2,1,0:T(8,128)(2,1)S(1)}, f32[184,1024]{1,0:T(8,128)S(1)}, f32[184,4096]{1,0...) custom-call(bf16[64,4096]{1,0:T(8,128)(2,1)S(1)} %bitcast.62, bf16[64,1024]{1,0:T(8,128)(2,1)S(1)} %bitcast.63, ...), custom_call_target="tpu_custom_call" | custom-call | bytes 100000000 | tf_op jit(solution)/shard_map/pallas_call | solution.py:435
  59.8 1.5 %fusion.11 = bf16[184,512]{1,0:T(8,128)(2,1)S(1)} fusion(bf16[512,4096]{1,0:T(8,128)(2,1)S(1)} %bitcast.51, bf16[184,4096]{1,0:T(8,128)(2,1)S(1)} %copy-done, s32[512]{0:T(512)S(1)} %fusion.16, s32[184]{0:T(256)S(1)} %add.91), kind=kOutput, calls=%fused_computation.22 | convolution fusion | flops 772034560 | bytes 5892832 | tf_op jit(solution)/shard_map/dot_general | solution.py:22
  61.4 0.5 fusion.9
  61.9 1.3 fusion.26
  63.2 0.5 fusion.27
  63.7 0.5 fusion.8
  64.2 2.1 %fusion.2 = bf16[184,4096]{1,0:T(8,128)(2,1)} fusion(bf16[184,512]{1,0:T(8,128)(2,1)S(1)} %fusion.8, bf16[512,4096]{1,0:T(8,128)(2,1)S(1)} %bitcast.52), kind=kOutput, calls=%fused_computation.5 | convolution fusion | flops 773259264 | bytes 5890048 | tf_op jit(solution)/shard_map/dot_general | solution.py:18
  66.3 1.5 %fusion.10 = bf16[184,512]{1,0:T(8,128)(2,1)S(1)} fusion(bf16[184,4096]{1,0:T(8,128)(2,1)S(1)} %get-tuple-element.15, bf16[512,4096]{1,0:T(8,128)(2,1)S(1)} %bitcast.53, s32[512]{0:T(512)S(1)} %fusion.16, s32[184]{0:T(256)S(1)} %bitcast.68), kind=kOutput, calls=%fused_computation.21 | convolution fusion | flops 772034560 | bytes 5892832 | tf_op jit(solution)/shard_map/dot_general | solution.py:22
  67.8 1.1 fusion.5
  68.9 2.0 %collective-permute-start.1 = (bf16[184,1024]{1,0:T(8,128)(2,1)}, bf16[184,1024]{1,0:T(8,128)(2,1)}, u32[]{:S(2)}, u32[]{:S(2)}) collective-permute-start(bf16[184,1024]{1,0:T(8,128)(2,1)} %fusion.5), channel_id=1, source_target_pairs={{0,2},{1,3},{2,0},{3,1},{4,6},{5,7},{6,4},{7,5},{8,10},{9,11},{10,... | collective-permute-start | bytes 1130504 | tf_op jit(solution)/shard_map/ppermute | solution.py:511
  71.0 1.4 add_convert_fusion
  72.3 0.5 add_convert_fusion.2
  72.8 59.4 %shard_map.103 = (bf16[64,4096]{1,0:T(8,128)(2,1)S(1)}, bf16[64,1024]{1,0:T(8,128)(2,1)S(1)}) custom-call(bf16[4,2,64,4096]{3,2,1,0:T(8,128)(2,1)S(1)} %bitcast.55, bf16[4,2,64,1024]{3,2,1,0:T(8,128)(2,1)S(1)} %bitcast.56), custom_call_target="tpu_custom_call" | custom-call | bytes 100000000 | tf_op jit(solution)/shard_map/pallas_call | solution.py:473
  132.2 2.2 %add_convert_fusion.3 = bf16[184,1024]{1,0:T(8,128)(2,1)} fusion(f32[184,1024]{1,0:T(8,128)S(1)} %get-tuple-element.12, bf16[184,1024]{1,0:T(8,128)(2,1)} %collective-permute-done.1, bf16[184,512]{1,0:T(8,128)(2,1)} %copy-done.4, bf16[512,1024]{1,0:T(8,128)(2,1)S(1)} %bitcast.60), kind=kOutput, calls=%fused_computation.23 | convolution fusion | flops 194256896 | bytes 2744320 | tf_op jit(solution)/shard_map/dot_general | solution.py:18
  134.4 2.3 %add_convert_fusion.1 = bf16[184,4096]{1,0:T(8,128)(2,1)} fusion(f32[184,4096]{1,0:T(8,128)S(1)} %get-tuple-element.16, bf16[184,4096]{1,0:T(8,128)(2,1)S(1)} %collective-permute-done.2, bf16[184,512]{1,0:T(8,128)(2,1)S(1)} %fusion.9, bf16[512,4096]{1,0:T(8,128)(2,1)S(1)} %bitcast.54), kind=kOutput, calls=%fused_computation.6 | convolution fusion | flops 777027584 | bytes 10412032 | tf_op jit(solution)/shard_map/dot_general | solution.py:18
  136.7 0.8 copy.13
  137.5 0.7 copy.14
  (11 shorter events, 0.0 us)
Async XLA Ops:
  2.0 61.7 %collective-permute-start = (s32[184,1]{0,1:T(1,128)S(1)}, s32[184,1]{0,1:T(1,128)S(1)}, u32[]{:S(2)}, u32[]{:S(2)}) collective-permute-start(s32[184,1]{0,1:T(1,128)S(1)} %bitcast.66), channel_id=1, source_target_pairs={{0,2},{1,3},{2,0},{3,1},{4,6},{5,7},{6,4},{7,5},{8,10},{9,11},{10,... | collective-permute-start | bytes 2216 | tf_op jit(solution)/shard_map/ppermute | solution.py:511
  5.0 1.4 %copy-start = (bf16[184,4096]{1,0:T(8,128)(2,1)S(1)}, bf16[184,4096]{1,0:T(8,128)(2,1)}, u32[]{:S(2)}) copy-start(bf16[184,4096]{1,0:T(8,128)(2,1)} %x.1) | copy-start | bytes 4521988
  6.4 1.0 copy-start.1
  7.3 1.0 copy-start.2
  8.4 0.9 copy-start.3
  61.4 1.8 %copy-start.4 = (bf16[184,512]{1,0:T(8,128)(2,1)}, bf16[184,512]{1,0:T(8,128)(2,1)S(1)}, u32[]{:S(2)}) copy-start(bf16[184,512]{1,0:T(8,128)(2,1)S(1)} %fusion.11) | copy-start | bytes 565252
  66.3 68.2 %collective-permute-start.2 = (bf16[184,4096]{1,0:T(8,128)(2,1)}, bf16[184,4096]{1,0:T(8,128)(2,1)S(1)}, u32[]{:S(2)}, u32[]{:S(2)}) collective-permute-start(bf16[184,4096]{1,0:T(8,128)(2,1)} %fusion.2), channel_id=1, source_target_pairs={{0,2},{1,3},{2,0},{3,1},{4,6},{5,7},{6,4},{7,5},{8,10},{9,11},{10,... | collective-permute-start | bytes 4521992 | tf_op jit(solution)/shard_map/ppermute | solution.py:511
  68.9 63.3 %collective-permute-start.1 = (bf16[184,1024]{1,0:T(8,128)(2,1)}, bf16[184,1024]{1,0:T(8,128)(2,1)}, u32[]{:S(2)}, u32[]{:S(2)}) collective-permute-start(bf16[184,1024]{1,0:T(8,128)(2,1)} %fusion.5), channel_id=1, source_target_pairs={{0,2},{1,3},{2,0},{3,1},{4,6},{5,7},{6,4},{7,5},{8,10},{9,11},{10,... | collective-permute-start | bytes 1130504 | tf_op jit(solution)/shard_map/ppermute | solution.py:511

commit v5 on v4

--- a/solution.py
+++ b/solution.py
@@ -319,9 +319,12 @@
         greet(barrier, in_column(k))
     pl.semaphore_wait(barrier, plane + layers - 2)
 
+    lower = z < layers // 2
     order = []
-    for i in range((layers + 1) // 2):
-        order += [layers - 1 - i, i] if layers - 1 - i != i else [i]
+    for i in range(layers // 2):
+        order += [jnp.where(lower, layers - 1 - i, i), jnp.where(lower, i, layers - 1 - i)]
+    if layers % 2:
+        order.append(layers // 2)
 
     def to_twin(j, a):
         part, got = arrays[a][:2]
@@ -332,12 +335,7 @@
         for a in range(2):
             to_twin(j, a).start()
 
-    ready = set()
-
     def prepare(j):
-        if j in ready:
-            return
-        ready.add(j)
         for a in range(2):
             part, got, total = arrays[a][:3]
             to_twin(j, a).wait_recv()
@@ -366,20 +364,19 @@
             out[way, j] = total[j].astype(bf16)
             hop(way, j, a).start()
 
-    lower = z < layers // 2
-
     def moves(way, j):
         return z < j if way == 0 else z > j
 
     for i in range(layers - 1):
         far, near = layers - 1 - i, i
-        prepare(far)
-        prepare(near)
+        if 2 * i < layers:
+            prepare(order[2 * i])
         pl.when(moves(0, far) & lower)(functools.partial(forward, 0, far))
-        pl.when(moves(1, near))(functools.partial(forward, 1, near))
+        pl.when(moves(1, near) & ~lower)(functools.partial(forward, 1, near))
+        if 2 * i + 1 < layers:
+            prepare(order[2 * i + 1])
+        pl.when(moves(1, near) & lower)(functools.partial(forward, 1, near))
         pl.when(moves(0, far) & ~lower)(functools.partial(forward, 0, far))
-    for j in range(layers):
-        prepare(j)
     for j in range(layers):
         if j > 0:
             pl.when(z == j)(functools.partial(take, 0, j))

time: 138 us -> 137 us (level)
  transfers between devices with their start and end apart: 3 -> 3, of which waited for: 0 -> 0; matrix products, arithmetic and copies ran while one was open for 8% -> 8% of each run, Pallas kernels for 80% -> 79%
where the time goes in v5:
time: 137 us
  Pallas kernels  109 us (80%)
  matrix products  15.3 us (11%)
  local copies, waits for them, and re-layouts  5.77 us (4%)
  starting transfers between devices  5 us (4%)
  other arithmetic  1.37 us (1%)
    pallas_call x1, Pallas kernels, reduce_line(): pl.pallas_call(functools.partial(reduce_kernel, layers, limit), out_shape...  58.3 us
    pallas_call x1, Pallas kernels, gather_line(): pl.pallas_call(functools.partial(gather_kernel, layers), out_shape=(jax.S...  50.5 us
    dot_general x4, matrix products, dot_nn(): lax.dot_general(a, b, (((1,), (0,)), ((), ())), preferred_element_type=f32)  7.65 us
    unnamed x12, local copies, waits for them, and re-layouts  5.77 us
    ppermute x3, starting transfers between devices, swap_line(): return lax.ppermute(v, 'dev', to_line)  5 us
    dot_general x4, matrix products, dot_nt(): lax.dot_general(a, b, (((1,), (1,)), ((), ())), preferred_element_type=f32)  4.09 us
    dot_general x4, matrix products, dot_tn(): lax.dot_general(a, b, (((0,), (0,)), ((), ())), preferred_element_type=f32)  3.6 us
  transfers between devices with their start and end apart: 3, of which 0 were waited for; matrix products, arithmetic and copies ran while one was open for 8% of the time, Pallas kernels for 79%

profile of v5, /device:TPU:0, one launch (start us, length us, event | category | flops | bytes accessed | tf_op | source)
XLA Modules:
  0.0 137.1 jit_solution(423465448933998047)
XLA Ops:
  0.6 0.7 broadcast_multiply_fusion
  1.3 0.7 add.91
  2.0 3.0 %collective-permute-start = (s32[184,1]{0,1:T(1,128)S(1)}, s32[184,1]{0,1:T(1,128)S(1)}, u32[]{:S(2)}, u32[]{:S(2)}) collective-permute-start(s32[184,1]{0,1:T(1,128)S(1)} %bitcast.66), channel_id=1, source_target_pairs={{0,2},{1,3},{2,0},{3,1},{4,6},{5,7},{6,4},{7,5},{8,10},{9,11},{10,... | collective-permute-start | bytes 2216 | tf_op jit(solution)/shard_map/ppermute | solution.py:508
  5.0 1.4 %copy-done = bf16[184,4096]{1,0:T(8,128)(2,1)S(1)} copy-done((bf16[184,4096]{1,0:T(8,128)(2,1)S(1)}, bf16[184,4096]{1,0:T(8,128)(2,1)}, u32[]{:S(2)}) %copy-start) | copy-done | bytes 1507352
  6.4 1.0 copy-done.1
  7.3 1.0 copy-done.2
  8.4 0.9 copy-done.3
  9.3 50.5 %shard_map.102 = (bf16[4,2,64,4096]{3,2,1,0:T(8,128)(2,1)S(1)}, bf16[4,2,64,1024]{3,2,1,0:T(8,128)(2,1)S(1)}, f32[184,1024]{1,0:T(8,128)S(1)}, f32[184,4096]{1,0...) custom-call(bf16[64,4096]{1,0:T(8,128)(2,1)S(1)} %bitcast.62, bf16[64,1024]{1,0:T(8,128)(2,1)S(1)} %bitcast.63, ...), custom_call_target="tpu_custom_call" | custom-call | bytes 100000000 | tf_op jit(solution)/shard_map/pallas_call | solution.py:432
  59.8 1.5 %fusion.11 = bf16[184,512]{1,0:T(8,128)(2,1)S(1)} fusion(bf16[512,4096]{1,0:T(8,128)(2,1)S(1)} %bitcast.51, bf16[184,4096]{1,0:T(8,128)(2,1)S(1)} %copy-done, s32[512]{0:T(512)S(1)} %fusion.16, s32[184]{0:T(256)S(1)} %add.91), kind=kOutput, calls=%fused_computation.22 | convolution fusion | flops 772034560 | bytes 5892832 | tf_op jit(solution)/shard_map/dot_general | solution.py:22
  61.4 0.5 fusion.9
  61.9 1.3 fusion.26
  63.2 0.5 fusion.27
  63.7 0.5 fusion.8
  64.2 2.1 %fusion.2 = bf16[184,4096]{1,0:T(8,128)(2,1)} fusion(bf16[184,512]{1,0:T(8,128)(2,1)S(1)} %fusion.8, bf16[512,4096]{1,0:T(8,128)(2,1)S(1)} %bitcast.52), kind=kOutput, calls=%fused_computation.5 | convolution fusion | flops 773259264 | bytes 5890048 | tf_op jit(solution)/shard_map/dot_general | solution.py:18
  66.3 1.5 %fusion.10 = bf16[184,512]{1,0:T(8,128)(2,1)S(1)} fusion(bf16[184,4096]{1,0:T(8,128)(2,1)S(1)} %get-tuple-element.15, bf16[512,4096]{1,0:T(8,128)(2,1)S(1)} %bitcast.53, s32[512]{0:T(512)S(1)} %fusion.16, s32[184]{0:T(256)S(1)} %bitcast.68), kind=kOutput, calls=%fused_computation.21 | convolution fusion | flops 772034560 | bytes 5892832 | tf_op jit(solution)/shard_map/dot_general | solution.py:22
  67.8 1.1 fusion.5
  68.9 2.0 %collective-permute-start.1 = (bf16[184,1024]{1,0:T(8,128)(2,1)}, bf16[184,1024]{1,0:T(8,128)(2,1)}, u32[]{:S(2)}, u32[]{:S(2)}) collective-permute-start(bf16[184,1024]{1,0:T(8,128)(2,1)} %fusion.5), channel_id=1, source_target_pairs={{0,2},{1,3},{2,0},{3,1},{4,6},{5,7},{6,4},{7,5},{8,10},{9,11},{10,... | collective-permute-start | bytes 1130504 | tf_op jit(solution)/shard_map/ppermute | solution.py:508
  71.0 1.4 add_convert_fusion
  72.3 0.5 add_convert_fusion.2
  72.8 58.3 %shard_map.103 = (bf16[64,4096]{1,0:T(8,128)(2,1)S(1)}, bf16[64,1024]{1,0:T(8,128)(2,1)S(1)}) custom-call(bf16[4,2,64,4096]{3,2,1,0:T(8,128)(2,1)S(1)} %bitcast.55, bf16[4,2,64,1024]{3,2,1,0:T(8,128)(2,1)S(1)} %bitcast.56), custom_call_target="tpu_custom_call" | custom-call | bytes 100000000 | tf_op jit(solution)/shard_map/pallas_call | solution.py:470
  131.1 2.2 %add_convert_fusion.3 = bf16[184,1024]{1,0:T(8,128)(2,1)} fusion(f32[184,1024]{1,0:T(8,128)S(1)} %get-tuple-element.12, bf16[184,1024]{1,0:T(8,128)(2,1)} %collective-permute-done.1, bf16[184,512]{1,0:T(8,128)(2,1)} %copy-done.4, bf16[512,1024]{1,0:T(8,128)(2,1)S(1)} %bitcast.60), kind=kOutput, calls=%fused_computation.23 | convolution fusion | flops 194256896 | bytes 2744320 | tf_op jit(solution)/shard_map/dot_general | solution.py:18
  133.3 2.3 %add_convert_fusion.1 = bf16[184,4096]{1,0:T(8,128)(2,1)} fusion(f32[184,4096]{1,0:T(8,128)S(1)} %get-tuple-element.16, bf16[184,4096]{1,0:T(8,128)(2,1)S(1)} %collective-permute-done.2, bf16[184,512]{1,0:T(8,128)(2,1)S(1)} %fusion.9, bf16[512,4096]{1,0:T(8,128)(2,1)S(1)} %bitcast.54), kind=kOutput, calls=%fused_computation.6 | convolution fusion | flops 777027584 | bytes 10412032 | tf_op jit(solution)/shard_map/dot_general | solution.py:18
  135.6 0.8 copy.13
  136.4 0.7 copy.14
  (11 shorter events, 0.0 us)
Async XLA Ops:
  2.0 61.7 %collective-permute-start = (s32[184,1]{0,1:T(1,128)S(1)}, s32[184,1]{0,1:T(1,128)S(1)}, u32[]{:S(2)}, u32[]{:S(2)}) collective-permute-start(s32[184,1]{0,1:T(1,128)S(1)} %bitcast.66), channel_id=1, source_target_pairs={{0,2},{1,3},{2,0},{3,1},{4,6},{5,7},{6,4},{7,5},{8,10},{9,11},{10,... | collective-permute-start | bytes 2216 | tf_op jit(solution)/shard_map/ppermute | solution.py:508
  5.0 1.4 %copy-start = (bf16[184,4096]{1,0:T(8,128)(2,1)S(1)}, bf16[184,4096]{1,0:T(8,128)(2,1)}, u32[]{:S(2)}) copy-start(bf16[184,4096]{1,0:T(8,128)(2,1)} %x.1) | copy-start | bytes 4521988
  6.4 1.0 copy-start.1
  7.3 1.0 copy-start.2
  8.4 0.9 copy-start.3
  61.4 1.8 %copy-start.4 = (bf16[184,512]{1,0:T(8,128)(2,1)}, bf16[184,512]{1,0:T(8,128)(2,1)S(1)}, u32[]{:S(2)}) copy-start(bf16[184,512]{1,0:T(8,128)(2,1)S(1)} %fusion.11) | copy-start | bytes 565252
  66.3 67.1 %collective-permute-start.2 = (bf16[184,4096]{1,0:T(8,128)(2,1)}, bf16[184,4096]{1,0:T(8,128)(2,1)S(1)}, u32[]{:S(2)}, u32[]{:S(2)}) collective-permute-start(bf16[184,4096]{1,0:T(8,128)(2,1)} %fusion.2), channel_id=1, source_target_pairs={{0,2},{1,3},{2,0},{3,1},{4,6},{5,7},{6,4},{7,5},{8,10},{9,11},{10,... | collective-permute-start | bytes 4521992 | tf_op jit(solution)/shard_map/ppermute | solution.py:508
  68.9 62.2 %collective-permute-start.1 = (bf16[184,1024]{1,0:T(8,128)(2,1)}, bf16[184,1024]{1,0:T(8,128)(2,1)}, u32[]{:S(2)}, u32[]{:S(2)}) collective-permute-start(bf16[184,1024]{1,0:T(8,128)(2,1)} %fusion.5), channel_id=1, source_target_pairs={{0,2},{1,3},{2,0},{3,1},{4,6},{5,7},{6,4},{7,5},{8,10},{9,11},{10,... | collective-permute-start | bytes 1130504 | tf_op jit(solution)/shard_map/ppermute | solution.py:508
